TPU v7x, 32 devices: a whole 2x2x4 slice. The times are simulated.
32 devices in a mesh: ctx: 16 (over z, x, core), head: 2 (over y).
Axes of the slice: x: 2, y: 2, z: 4, core: 2. Of those that a mesh axis runs over, the one named last changes fastest.
Arguments:
- queries: bfloat16 [2048, 36864], P('ctx', 'head'), may hold values from -6 to 6
- latents: bfloat16 [4096, 576], P('ctx'), may hold values from -5 to 5
- up_value: bfloat16 [512, 8192], P(None, 'head'), may hold values from -0.25 to 0.25
- grad_out: bfloat16 [2048, 8192], P('ctx', 'head'), may hold values from -12 to 12
- out_saved: bfloat16 [2048, 8192], P('ctx', 'head'), may hold values from -6 to 6
- log_sums: float32 [2048, 64], P('ctx', 'head'), as said below
- doc_starts: int32 [65], replicated, may hold values from 0 to 4096, as said below
Outputs:
- grad_queries: bfloat16 [2048, 36864], P('ctx', 'head')
- grad_latents: float32 [4096, 576], P(('ctx', 'head'))
- grad_up_value: float32 [512, 8192], P('ctx', 'head')
Inputs may be any that keep to these rules, and one draw needn't show every extreme that they name: doc_starts[0] is 0; the entries rise strictly until they reach 4096 and then stay at 4096; consecutive entries differ by at most 512, and some document has exactly 512 positions. log_sums[t, h] is the log of the sum of exp(score[t, h, s]) over the keys s allowed for query t, computed from these queries and latents.
All inputs are finite; a program needn't handle non-finite values.
Results may differ from a plain program's by a relative error of at most 0.0085.
Values may be sent and summed in bfloat16 or wider, within the bound.
No kernel may reach another device: no remote copies, remote signals or barrier semaphores. Data moves between devices by JAX's collectives and lax.ppermute only.
A program may use at most 128 MiB of HBM per device.

v0:
```python
import functools

import jax
import jax.numpy as jnp
from jax import lax
from jax.experimental import pallas as pl
from jax.experimental.pallas import tpu as pltpu
from jax.sharding import PartitionSpec as P

softmax_scale = 192.0 ** (-0.5)
vmem_bytes = 32 * 1024 * 1024
prepare_bytes = 54 * 1024 * 1024
small_bytes = 16 * 1024 * 1024
chunks = 2
pieces = 2


def nt_dot(a, b):
    return lax.dot_general(a, b, (((1,), (1,)), ((), ())), preferred_element_type=jnp.float32)


def nn_dot(a, b):
    return lax.dot_general(a, b, (((1,), (0,)), ((), ())), preferred_element_type=jnp.float32)


def beside_heads(ref, heads, width):
    return jnp.concatenate([ref[:, h * width : (h + 1) * width] for h in heads], axis=1)


def on_diagonal(ref, heads, width):
    blocks = [ref[:, h * width : (h + 1) * width] for h in heads]
    zero = jnp.zeros_like(blocks[0])
    return jnp.concatenate(
        [
            jnp.concatenate([block if i == j else zero for j in range(len(blocks))], axis=1)
            for i, block in enumerate(blocks)
        ],
        axis=0,
    )


def pairs_of(unit, per_unit):
    heads = list(range(unit * per_unit, (unit + 1) * per_unit))
    return [heads[i : i + 2] for i in range(0, per_unit, 2)]


def wide_rows(q_ref, heads, feat, width):
    parts = []
    for head in heads:
        if head * feat % 128 == 0:
            parts.append(q_ref[:, head * feat : head * feat + width])
        else:
            end = (head + 1) * feat
            wide = q_ref[:, end - width : end]
            parts.append(jnp.concatenate([wide[:, width - feat :], wide[:, : width - feat]], axis=1))
    return jnp.concatenate(parts, axis=0)


def prepare_kernel(
    place_ref, docs_ref, lat_ref, lse_ref, q_ref, g_ref, o_ref, w_ref,
    own_ref, table_ref, qs_ref, glat_ref, *, units, per_unit, rows, feat, vdim, key_rows,
):
    heads = lse_ref.shape[0]
    window = table_ref.shape[0] - 2 * heads
    width = qs_ref.shape[1]
    span = per_unit * rows

    @pl.when(pl.program_id(0) == 0)
    def _():
        own_ref[...] = lat_ref[...]
        table_ref[window : window + heads, :] = lse_ref[...]
        place = place_ref[0]
        query_pos = place * key_rows + (key_rows - rows) + lax.broadcasted_iota(jnp.int32, (8, rows), 1)
        start = jnp.zeros((8, rows), jnp.int32)
        for i in range(docs_ref.shape[0]):
            entry = docs_ref[i]
            start = jnp.where(entry <= query_pos, jnp.maximum(start, entry), start)
        key_pos = (place + 1) * key_rows - window + lax.broadcasted_iota(jnp.int32, (window, rows), 0)
        allowed = (key_pos >= start[:1]) & (key_pos <= query_pos[:1])
        table_ref[:window, :] = jnp.where(allowed, 0.0, -1e30)

    deltas = []
    for unit in range(units):
        pairs = pairs_of(unit, per_unit)
        qs_ref[unit * span : (unit + 1) * span, :] = wide_rows(q_ref, sum(pairs, []), feat, width)
        for i, pair in enumerate(pairs):
            row = unit * span + 2 * i * rows
            glat_ref[row : row + 2 * rows, :] = nt_dot(
                on_diagonal(g_ref, pair, vdim), beside_heads(w_ref, pair, vdim)
            ).astype(glat_ref.dtype)
            for head in pair:
                lanes = slice(head * vdim, (head + 1) * vdim)
                product = g_ref[:, lanes].astype(jnp.float32) * o_ref[:, lanes].astype(jnp.float32)
                deltas.append(jnp.sum(product.T, axis=0, keepdims=True))
    count = len(deltas)
    row = window + heads + pl.program_id(0) * count
    table_ref[pl.ds(pl.multiple_of(row, count), count), :] = jnp.concatenate(deltas, axis=0)


def forward_kernel(
    place_ref, *rest, units, per_unit, rows, feat, lat, vdim, base, own_rows, first, key_rows,
):
    if first:
        (lat0_ref, lat1_ref, lat2_ref, qs_ref, g_ref, table_ref, p_ref, keep_ref, send_ref, ct_ref, c_ref) = rest
    else:
        (ct_ref, c_ref, qs_ref, g_ref, table_ref, _, p_ref, keep_ref, send_ref) = rest
    window, width = c_ref.shape
    far = window - key_rows
    core = place_ref[0] % 2

    if first:

        @pl.when(pl.program_id(0) == 0)
        def _():
            ct_ref[:, : far - key_rows] = lat2_ref[...]
            ct_ref[:, far - key_rows : far] = lat1_ref[...]
            ct_ref[:, far:] = lat0_ref[...]
            gap = jnp.zeros((width - feat, window), ct_ref.dtype)
            c_ref[...] = jnp.concatenate([ct_ref[...], gap], axis=0).T

    bias = table_ref[:window, :]
    span = per_unit * rows
    scores = [nt_dot(c_ref[...], qs_ref[unit * span : (unit + 1) * span, :]) for unit in range(units)]
    for unit in range(units):
        for k in range(per_unit):
            index = ((pl.program_id(0) + base) * units + unit) * per_unit + k
            shift = table_ref[pl.ds(window + index, 1), :]
            column = unit * span + k * rows
            p_ref[:, column : column + rows] = jnp.exp(
                scores[unit][:, k * rows : (k + 1) * rows] * softmax_scale + (bias - shift)
            ).astype(jnp.bfloat16)
    olats = [
        nn_dot(ct_ref[:lat, :], p_ref[:, unit * span : (unit + 1) * span]).astype(jnp.bfloat16)
        for unit in range(units)
    ]
    for unit in range(units):
        for i, pair in enumerate(pairs_of(unit, per_unit)):
            part = nn_dot(
                olats[unit][:, 2 * i * rows : 2 * (i + 1) * rows], on_diagonal(g_ref, pair, vdim)
            )
            lanes = slice(pair[0] * vdim, (pair[0] + 2) * vdim)
            part = part.reshape(lat // (2 * own_rows), 2, own_rows, 2 * vdim)
            low, high = part[:, 0], part[:, 1]
            keep_ref[:, lanes] = (
                jnp.where(core == 0, low, high).reshape(lat // 2, 2 * vdim).astype(keep_ref.dtype)
            )
            send_ref[:, lanes] = (
                jnp.where(core == 0, high, low).reshape(lat // 2, 2 * vdim).astype(send_ref.dtype)
            )


def backward_kernel(
    c_ref, qs_ref, glat_ref, table_ref, p_ref, *rest,
    units, per_unit, rows, feat, lat, steps, base, first, last, ties, key_rows,
):
    rest = list(rest)
    acc_in = None if first else rest.pop(0)
    rest = rest[ties:]
    ds_ref = rest.pop(0)
    if last:
        near_ref, far1_ref, far2_ref, acc = rest
    else:
        acc_out, acc = rest
    span = per_unit * rows

    @pl.when(pl.program_id(0) == 0)
    def _():
        acc[...] = jnp.zeros_like(acc) if first else acc_in[...]

    first_delta = (table_ref.shape[0] + c_ref.shape[0]) // 2
    gprobs = [
        nt_dot(c_ref[:, :lat], glat_ref[unit * span : (unit + 1) * span, :]) for unit in range(units)
    ]
    for unit in range(units):
        for k in range(per_unit):
            index = ((pl.program_id(0) + base) * units + unit) * per_unit + k
            delta = table_ref[pl.ds(first_delta + index, 1), :]
            own = slice(unit * span + k * rows, unit * span + (k + 1) * rows)
            ds_ref[:, own] = (
                p_ref[:, own].astype(jnp.float32)
                * ((gprobs[unit][:, k * rows : (k + 1) * rows] - delta) * softmax_scale)
            ).astype(jnp.bfloat16)
    acc[:, :lat] += nn_dot(
        jnp.concatenate([ds_ref[...], p_ref[...]], axis=1),
        jnp.concatenate([qs_ref[:, :lat], glat_ref[...]], axis=0),
    )
    acc[:, lat:] += nn_dot(ds_ref[...], qs_ref[:, lat:])

    @pl.when(pl.program_id(0) == steps - 1)
    def _():
        if last:
            far2 = far2_ref.shape[1]
            total = acc[...].T[:feat]
            far2_ref[...] = total[:, :far2].astype(far2_ref.dtype)
            far1_ref[...] = total[:, far2 : far2 + key_rows].astype(far1_ref.dtype)
            near_ref[...] = total[:, far2 + key_rows :]
        else:
            acc_out[...] = acc[...]


def query_kernel(ct_ref, ds_ref, *rest, pairs, rows, feat):
    gq_ref, token_ref = rest[-2:]
    token_ref[...] = jnp.zeros_like(token_ref)
    turned = nn_dot(ct_ref[...], ds_ref[...]).astype(jnp.bfloat16)
    for i in range(pairs):
        both = jnp.concatenate(
            [turned[:, (2 * i + j) * rows : (2 * i + j + 1) * rows] for j in range(2)], axis=0
        )
        gq_ref[:, 2 * i * feat : 2 * (i + 1) * feat] = both.T


def passed_along(value, axis, steps):
    count = lax.axis_size(axis)
    first, last = (max(0, -steps), min(count, count - steps))
    return lax.ppermute(value, axis, [(source, source + steps) for source in range(first, last)])


def swapped(value, axis, bit):
    count = lax.axis_size(axis)
    return lax.ppermute(value, axis, [(source, source ^ bit) for source in range(count)])


def params(limit=vmem_bytes):
    return pltpu.CompilerParams(dimension_semantics=("arbitrary",), vmem_limit_bytes=limit)


def cost(flops, moved):
    return pl.CostEstimate(flops=int(flops / 8), bytes_accessed=int(moved), transcendentals=0)


def bit_of(place, bit):
    return (place >> bit) & 1


def halving_kernel(place_ref, hold_ref, got_ref, send_ref, keep_ref, *, dim, bit):
    mine = bit_of(place_ref[0], bit)
    lead = (slice(None),) * dim
    for which, out_ref in ((1 - mine, send_ref), (mine, keep_ref)):
        where = lead + (which,)
        out_ref[...] = (hold_ref[where].astype(jnp.float32) + got_ref[where].astype(jnp.float32)).astype(
            out_ref.dtype
        )


def final_kernel(hold_ref, got_ref, *refs):
    out_ref, lat_ref = refs[-2:]
    lat_ref[...] = hold_ref[...] + got_ref[...].astype(jnp.float32)
    cols = refs[0].shape[-1]
    for i in range(len(refs) // 2 - 1):
        out_ref[:, i * cols : (i + 1) * cols] = refs[2 * i][...] + refs[2 * i + 1][...].astype(jnp.float32)


def latent_kernel(side_ref, near_ref, got1_ref, got2_ref, _, send_ref, hold_ref):
    low = near_ref[...] + got1_ref[...].astype(jnp.float32)
    part = send_ref.shape[1]
    spare = near_ref.shape[1] - got2_ref.shape[1]
    whole = jnp.concatenate([low[:, :spare], low[:, spare:] + got2_ref[...].astype(jnp.float32)], axis=1)
    first, second = whole[:, :part], whole[:, part:]
    lower = side_ref[0] == 0
    send_ref[...] = jnp.where(lower, second, first).astype(send_ref.dtype)
    hold_ref[...] = jnp.where(lower, first, second)


class Halving:
    def __init__(self, hold, got, bits, place, axis):
        self.hold, self.got, self.place, self.axis = hold, got, place, axis
        self.opened, self.order = sorted(bits, reverse=True), list(bits)

    def step(self):
        bit = self.order.pop(0)
        shape = (2,) * (len(self.opened) - 1) + self.hold.shape[-2:]
        vmem = pl.BlockSpec(memory_space=pltpu.VMEM)
        sent, self.hold = pl.pallas_call(
            functools.partial(halving_kernel, dim=self.opened.index(bit), bit=bit),
            in_specs=[pl.BlockSpec(memory_space=pltpu.SMEM), vmem, vmem],
            out_shape=[jax.ShapeDtypeStruct(shape, jnp.bfloat16), jax.ShapeDtypeStruct(shape, jnp.float32)],
            compiler_params=pltpu.CompilerParams(vmem_limit_bytes=small_bytes),
            cost_estimate=cost(1e6, 2e6),
            name="halving",
        )(self.place, self.hold, self.got)
        self.opened.remove(bit)
        self.got = swapped(sent.reshape((-1, shape[-1])), self.axis, 1 << bit).reshape(shape)
        return sent


def on_device(queries, latents, up_value, grad_out, out_saved, log_sums, doc_starts):
    rows = queries.shape[0]
    key_rows, feat = latents.shape
    lat = up_value.shape[0]
    heads = log_sums.shape[1]
    vdim = grad_out.shape[1] // heads
    ctx = lax.axis_size("ctx")
    own_rows = lat // ctx
    window = 2 * key_rows + rows
    far = window - key_rows
    width = -(-feat // 128) * 128
    unit = max(2, min(4, heads // pieces))

    place = lax.axis_index("ctx").astype(jnp.int32)
    turned = latents.T
    prev1 = passed_along(turned, "ctx", 1)
    prev2 = passed_along(turned[:, key_rows - (far - key_rows) :], "ctx", 2)
    sums_turned = log_sums.T

    def whole(*shape):
        return pl.BlockSpec(shape, lambda i: (0,) * len(shape))

    smem = pl.BlockSpec(memory_space=pltpu.SMEM)
    untouched = pl.BlockSpec(memory_space=pl.ANY)
    scalar = place.reshape(1)

    chunk_heads = heads // chunks
    units = max(1, min(2, heads // unit))
    group = units * unit
    lanes = lambda i: (0, i)
    rowed = lambda i: (i, 0)
    own, table, stacked, glat = pl.pallas_call(
        functools.partial(
            prepare_kernel, units=units, per_unit=unit, rows=rows, feat=feat, vdim=vdim, key_rows=key_rows
        ),
        grid=(heads // group,),
        in_specs=[
            smem,
            smem,
            whole(feat, key_rows),
            whole(heads, rows),
            pl.BlockSpec((rows, group * feat), lanes),
            pl.BlockSpec((rows, group * vdim), lanes),
            pl.BlockSpec((rows, group * vdim), lanes),
            pl.BlockSpec((lat, group * vdim), lanes),
        ],
        out_specs=[
            whole(feat, key_rows),
            whole(window + 2 * heads, rows),
            pl.BlockSpec((group * rows, width), rowed),
            pl.BlockSpec((group * rows, lat), rowed),
        ],
        out_shape=[
            jax.ShapeDtypeStruct((feat, key_rows), jnp.bfloat16),
            jax.ShapeDtypeStruct((window + 2 * heads, rows), jnp.float32),
            jax.ShapeDtypeStruct((heads * rows, width), jnp.bfloat16),
            jax.ShapeDtypeStruct((heads * rows, lat), jnp.bfloat16),
        ],
        compiler_params=params(prepare_bytes),
        cost_estimate=cost(heads * rows * 4 * lat * vdim, 20e6),
        name="prepare",
    )(scalar, doc_starts, turned, sums_turned, queries, grad_out, out_saved, up_value)

    probs = None
    partials = []
    units = max(1, min(2, chunk_heads // unit))
    group = units * unit
    steps = chunk_heads // group
    for chunk in range(chunks):
        base = chunk * steps
        lanes = lambda i, base=base: (0, i + base)
        rowed = lambda i, base=base: (i + base, 0)
        first = chunk == 0
        in_specs = [smem]
        operands = [scalar]
        if first:
            in_specs += [whole(feat, key_rows), whole(feat, key_rows), whole(feat, far - key_rows)]
            operands += [own, prev1, prev2]
        else:
            in_specs += [whole(feat, window), whole(window, width)]
            operands += [keys_turned, keys]
        in_specs += [
            pl.BlockSpec((group * rows, width), rowed),
            pl.BlockSpec((rows, group * vdim), lanes),
            whole(window + 2 * heads, rows),
        ]
        operands += [stacked, grad_out, table]
        halves = [pl.BlockSpec((lat // 2, group * vdim), lambda i: (0, i))] * 2
        out_specs = [pl.BlockSpec((window, group * rows), lanes)] + halves
        out_shape = [jax.ShapeDtypeStruct((window, heads * rows), jnp.bfloat16)]
        out_shape += [jax.ShapeDtypeStruct((lat // 2, chunk_heads * vdim), jnp.bfloat16)] * 2
        aliases = {}
        if first:
            out_specs += [whole(feat, window), whole(window, width)]
            out_shape += [
                jax.ShapeDtypeStruct((feat, window), jnp.bfloat16),
                jax.ShapeDtypeStruct((window, width), jnp.bfloat16),
            ]
        else:
            aliases = {len(operands): 0}
            in_specs.append(untouched)
            operands.append(probs)
        out = pl.pallas_call(
            functools.partial(
                forward_kernel, units=units, per_unit=unit, rows=rows, feat=feat, lat=lat, vdim=vdim,
                base=base, own_rows=own_rows, first=first, key_rows=key_rows,
            ),
            grid=(steps,),
            in_specs=in_specs,
            out_specs=out_specs,
            out_shape=out_shape,
            input_output_aliases=aliases,
            compiler_params=params(),
            cost_estimate=cost(chunk_heads * rows * 2 * window * (width + lat) * 2, 1e6),
            name="forward",
        )(*operands)
        if first:
            keys_turned, keys = out[3:]
        probs, keep, send = out[:3]
        partials.append((keep, send))

    upper = list(range(1, ctx.bit_length() - 1))
    shape = (2,) * len(upper) + (own_rows, chunk_heads * vdim)
    halvings = []
    for (keep, send), order in zip(partials, (upper[1:] + upper[:1], upper)):
        got = swapped(send, "ctx", 1)
        halvings.append(Halving(keep.reshape(shape), got.reshape(shape), order, scalar, "ctx"))

    piece_heads = heads // pieces
    units = max(1, min(2, piece_heads // unit))
    group = units * unit
    steps = piece_heads // group
    acc = None
    for piece in range(pieces):
        ties = [halving.step() for halving in halvings if halving.order]
        first, last = piece == 0, piece == pieces - 1
        base = piece * steps
        lanes = lambda i, base=base: (0, i + base)
        rowed = lambda i, base=base: (i + base, 0)
        in_specs = [
            whole(window, width),
            pl.BlockSpec((group * rows, width), rowed),
            pl.BlockSpec((group * rows, lat), rowed),
            whole(window + 2 * heads, rows),
            pl.BlockSpec((window, group * rows), lanes),
        ]
        operands = [keys, stacked, glat, table, probs]
        if not first:
            in_specs.append(whole(window, width))
            operands.append(acc)
        in_specs += [untouched] * len(ties)
        operands += ties
        out_specs = [pl.BlockSpec((window, group * rows), lanes)]
        out_shape = [jax.ShapeDtypeStruct((window, heads * rows), jnp.bfloat16)]
        if last:
            out_specs += [whole(feat, key_rows), whole(feat, key_rows), whole(feat, far - key_rows)]
            out_shape += [
                jax.ShapeDtypeStruct((feat, key_rows), jnp.float32),
                jax.ShapeDtypeStruct((feat, key_rows), jnp.bfloat16),
                jax.ShapeDtypeStruct((feat, far - key_rows), jnp.bfloat16),
            ]
        else:
            out_specs.append(whole(window, width))
            out_shape.append(jax.ShapeDtypeStruct((window, width), jnp.float32))
        probs, *rest = pl.pallas_call(
            functools.partial(
                backward_kernel, units=units, per_unit=unit, rows=rows, feat=feat, lat=lat, base=base,
                steps=steps, first=first, last=last, ties=len(ties), key_rows=key_rows,
            ),
            grid=(steps,),
            in_specs=in_specs,
            out_specs=out_specs,
            out_shape=out_shape,
            scratch_shapes=[pltpu.VMEM((window, width), jnp.float32)],
            input_output_aliases={4: 0},
            compiler_params=params(),
            cost_estimate=cost(piece_heads * rows * 2 * window * (width + 2 * lat) * 2, 1e6),
            name="backward",
        )(*operands)
        if last:
            near, far1, far2 = rest
        else:
            (acc,) = rest
    dscores = probs

    def query_gradient(piece, so_far, ties):
        base = piece * steps
        lanes = lambda i: (0, i + base)
        extra = ([] if so_far is None else [so_far]) + ties
        return pl.pallas_call(
            functools.partial(query_kernel, pairs=group // 2, rows=rows, feat=feat),
            grid=(steps,),
            in_specs=[whole(feat, window), pl.BlockSpec((window, group * rows), lanes)] + [untouched] * len(extra),
            out_specs=[pl.BlockSpec((rows, group * feat), lanes), whole(8, 128)],
            out_shape=[
                jax.ShapeDtypeStruct(queries.shape, jnp.bfloat16),
                jax.ShapeDtypeStruct((8, 128), jnp.float32),
            ],
            input_output_aliases={} if so_far is None else {2: 0},
            compiler_params=params(),
            cost_estimate=cost(piece_heads * rows * 2 * window * width * 3, 1e6),
            name="query_gradient",
        )(keys_turned, dscores, *extra)

    got1 = passed_along(far1, "ctx", -1)
    got2 = passed_along(far2, "ctx", -2)
    ties = [halving.step() for halving in halvings if halving.order]
    grad_queries, token = query_gradient(0, None, ties)
    position = lax.axis_index("head").astype(jnp.int32)
    bit = lax.axis_size("head") // 2
    part = key_rows // 2
    send, hold = pl.pallas_call(
        latent_kernel,
        in_specs=[smem] + [pl.BlockSpec(memory_space=pltpu.VMEM)] * 3 + [untouched],
        out_shape=[
            jax.ShapeDtypeStruct((feat, part), jnp.bfloat16),
            jax.ShapeDtypeStruct((feat, part), jnp.float32),
        ],
        compiler_params=pltpu.CompilerParams(vmem_limit_bytes=small_bytes),
        cost_estimate=cost(1e6, 2e6),
        name="latent",
    )((position // bit % 2).reshape(1), near, got1, got2, token)
    got = swapped(send, "head", bit)
    ties = [send] + [halving.got for halving in halvings]
    grad_queries, _ = query_gradient(1, grad_queries, ties)
    for halving in halvings:
        while halving.order:
            halving.step()
    while bit > 1:
        total = hold + got.astype(jnp.float32)
        bit //= 2
        part //= 2
        mine = (position // bit) % 2
        send = lax.dynamic_slice_in_dim(total, (1 - mine) * part, part, 1).astype(jnp.bfloat16)
        hold = lax.dynamic_slice_in_dim(total, mine * part, part, 1)
        got = swapped(send, "head", bit)
    vmem = pl.BlockSpec(memory_space=pltpu.VMEM)
    terms = sum(([halving.hold, halving.got] for halving in halvings), [])
    grad_up_value, turned_latents = pl.pallas_call(
        final_kernel,
        in_specs=[vmem] * (2 + len(terms)),
        out_shape=[
            jax.ShapeDtypeStruct((own_rows, heads * vdim), jnp.float32),
            jax.ShapeDtypeStruct((feat, part), jnp.float32),
        ],
        compiler_params=pltpu.CompilerParams(vmem_limit_bytes=small_bytes),
        cost_estimate=cost(1e6, 2e6),
        name="final",
    )(hold, got, *terms)
    return (grad_queries, turned_latents.T, grad_up_value)


def solution(mesh):
    return jax.shard_map(
        on_device,
        mesh=mesh,
        in_specs=(
            P("ctx", "head"),
            P("ctx", None),
            P(None, "head"),
            P("ctx", "head"),
            P("ctx", "head"),
            P("ctx", "head"),
            P(),
        ),
        out_specs=(P("ctx", "head"), P(("ctx", "head"), None), P("ctx", "head")),
        check_vma=False,
    )
```

profile of v0, /device:TPU:0, one launch (start us, length us, event | category | flops | bytes accessed | tf_op | source)
XLA Modules:
  0.0 86.3 jit_solution(1794752237567337596)
XLA Ops:
  0.6 2.4 %collective-permute-start = (bf16[576,256]{1,0:T(8,128)(2,1)}, bf16[576,256]{1,0:T(8,128)(2,1)S(1)}, u32[]{:S(2)}, u32[]{:S(2)}) collective-permute-start(bf16[576,256]{1,0:T(8,128)(2,1)} %bitcast.30), channel_id=1, source_target_pairs={{0,2},{2,4},{4,6},{6,8},{8,10},{10,12},{12,14},{14,16},{16,18},{18... | collective-permute-start | bytes 884744 | tf_op jit(solution)/shard_map/ppermute | solution.py:215
  3.0 0.9 %slice.4 = bf16[576,128]{1,0:T(8,128)(2,1)S(1)} slice(bf16[576,256]{1,0:T(8,128)(2,1)} %bitcast.31), slice={[0:576], [128:256]} | slice | bytes 294912 | tf_op jit(solution)/shard_map/slice | solution.py:302
  3.9 4.4 %collective-permute-start.1 = (bf16[576,128]{1,0:T(8,128)(2,1)S(1)}, bf16[576,128]{1,0:T(8,128)(2,1)S(1)}, u32[]{:S(2)}, u32[]{:S(2)}) collective-permute-start(bf16[576,128]{1,0:T(8,128)(2,1)S(1)} %slice.4), channel_id=1, source_target_pairs={{0,4},{2,6},{4,8},{6,10},{8,12},{10,14},{12,16},{14,18},{16,20},{1... | collective-permute-start | bytes 442376 | tf_op jit(solution)/shard_map/ppermute | solution.py:215
  8.4 9.0 %prepare.1 = (bf16[576,256]{1,0:T(8,128)(2,1)}, f32[704,128]{1,0:T(8,128)}, bf16[4096,640]{1,0:T(8,128)(2,1)}, bf16[4096,512]{1,0:T(8,128)(2,1)}) custom-call(s32[1]{0:T(128)} %bitcast.place_ref, s32[65]{0:T(128)} %docs_ref.1, bf16[576,256]{1,0:T(8,128)(2,1)} %bitcast.32, f32[32,128]{1,0:T(8,128)} %bitcast.33, bf16[128,18432]{1,0:T(8,128)(2,1)} %q_ref.1, ...), custom_call_target="tpu_custom_call" | custom-call | flops 134217728 | bytes 20000000 | tf_op jit(solution)/shard_map/prepare/pallas_call | solution.py:317
  17.4 2.5 %copy-done.2 = bf16[4096,640]{1,0:T(8,128)(2,1)S(1)} copy-done((bf16[4096,640]{1,0:T(8,128)(2,1)S(1)}, bf16[4096,640]{1,0:T(8,128)(2,1)}, u32[]{:S(2)}) %copy-start.2) | copy-done | bytes 5242904
  19.9 1.0 %copy-done.5 = f32[704,128]{1,0:T(8,128)S(1)} copy-done((f32[704,128]{1,0:T(8,128)S(1)}, f32[704,128]{1,0:T(8,128)}, u32[]{:S(2)}) %copy-start.5) | copy-done | bytes 360472
  20.9 1.0 %copy-done.7 = bf16[576,256]{1,0:T(8,128)(2,1)S(1)} copy-done((bf16[576,256]{1,0:T(8,128)(2,1)S(1)}, bf16[576,256]{1,0:T(8,128)(2,1)}, u32[]{:S(2)}) %copy-start.7) | copy-done | bytes 294936
  21.8 5.5 %forward.2 = (bf16[640,4096]{1,0:T(8,128)(2,1)S(1)}, bf16[256,2048]{1,0:T(8,128)(2,1)S(1)}, bf16[256,2048]{1,0:T(8,128)(2,1)S(1)}, bf16[576,640]{1,0:T(8,128)(2,1)S(1)}, bf16[640,640]{1,0:T(8,128)(2,1)S(1)}) custom-call(s32[1]{0:T(128)} %bitcast.place_ref, bf16[576,256]{1,0:T(8,128)(2,1)S(1)} %copy-done.7, ...), custom_call_target="tpu_custom_call" | custom-call | flops 754974720 | bytes 1000000 | tf_op jit(solution)/shard_map/forward/pallas_call | solution.py:388
  27.4 5.2 %forward.3 = (bf16[640,4096]{1,0:T(8,128)(2,1)S(1)}, bf16[256,2048]{1,0:T(8,128)(2,1)S(1)}, bf16[256,2048]{1,0:T(8,128)(2,1)S(1)}) custom-call(s32[1]{0:T(128)} %bitcast.place_ref, bf16[576,640]{1,0:T(8,128)(2,1)S(1)} %get-tuple-element.43.rest_0_.ct_ref, bf16[640,640]{1,0:T(8,128)(2,1)S(1)} %get-tuple-element.44.rest_1_.c_ref, ...), custom_call_target="tpu_custom_call", output_to_operand_aliasing={{0}: (6, {})} | custom-call | flops 754974720 | bytes 1000000 | tf_op jit(solution)/shard_map/forward/pallas_call | solution.py:388
  32.6 1.4 %collective-permute-start.3 = (bf16[256,2048]{1,0:T(8,128)(2,1)S(1)}, bf16[256,2048]{1,0:T(8,128)(2,1)S(1)}, u32[]{:S(2)}, u32[]{:S(2)}) collective-permute-start(bf16[256,2048]{1,0:T(8,128)(2,1)S(1)} %get-tuple-element.52), channel_id=1, source_target_pairs={{0,2},{2,0},{4,6},{6,4},{8,10},{10,8},{12,14},{14,12},{16,18},{18,... | collective-permute-start | bytes 3145736 | tf_op jit(solution)/shard_map/ppermute | solution.py:220
  34.1 2.2 %collective-permute-done.3 = bf16[256,2048]{1,0:T(8,128)(2,1)S(1)} collective-permute-done((bf16[256,2048]{1,0:T(8,128)(2,1)S(1)}, bf16[256,2048]{1,0:T(8,128)(2,1)S(1)}, u32[]{:S(2)}, u32[]{:S(2)}) %collective-permute-start.3) | collective-permute-done | bytes 1048608 | tf_op jit(solution)/shard_map/ppermute | solution.py:220
  36.3 0.2 halving.7
  36.6 1.6 %collective-permute-start.5 = (bf16[128,2048]{1,0:T(8,128)(2,1)S(1)}, bf16[128,2048]{1,0:T(8,128)(2,1)S(1)}, u32[]{:S(2)}, u32[]{:S(2)}) collective-permute-start(bf16[128,2048]{1,0:T(8,128)(2,1)S(1)} %bitcast.23), channel_id=1, source_target_pairs={{0,4},{2,6},{4,0},{6,2},{8,12},{10,14},{12,8},{14,10},{16,20},{18,... | collective-permute-start | bytes 1572872 | tf_op jit(solution)/shard_map/ppermute | solution.py:220
  38.1 0.2 halving.6
  38.4 1.6 %collective-permute-start.4 = (bf16[128,2048]{1,0:T(8,128)(2,1)S(1)}, bf16[128,2048]{1,0:T(8,128)(2,1)S(1)}, u32[]{:S(2)}, u32[]{:S(2)}) collective-permute-start(bf16[128,2048]{1,0:T(8,128)(2,1)S(1)} %bitcast.24), channel_id=1, source_target_pairs={{0,8},{2,10},{4,12},{6,14},{8,0},{10,2},{12,4},{14,6},{16,24},{18,... | collective-permute-start | bytes 1572872 | tf_op jit(solution)/shard_map/ppermute | solution.py:220
  40.0 5.9 %backward.2 = (bf16[640,4096]{1,0:T(8,128)(2,1)S(1)}, f32[640,640]{1,0:T(8,128)S(1)}) custom-call(bf16[640,640]{1,0:T(8,128)(2,1)S(1)} %get-tuple-element.44.rest_1_.c_ref, bf16[4096,640]{1,0:T(8,128)(2,1)S(1)} %bitcast.18, bf16[4096,512]{1,0:T(8,128)(2,1)S(1)} %copy-done.3, f32[704,128]{1,0:T(8,128)S(1)} %copy-done.6, ...), custom_call_target="tpu_custom_call", output_to_operand_aliasing={{0}: (4, {})} | custom-call | flops 1090519040 | bytes 1000000 | tf_op jit(solution)/shard_map/backward/pallas_call | solution.py:450
  45.9 5.0 %collective-permute-done.5 = bf16[128,2048]{1,0:T(8,128)(2,1)S(1)} collective-permute-done((bf16[128,2048]{1,0:T(8,128)(2,1)S(1)}, bf16[128,2048]{1,0:T(8,128)(2,1)S(1)}, u32[]{:S(2)}, u32[]{:S(2)}) %collective-permute-start.5) | collective-permute-done | bytes 524320 | tf_op jit(solution)/shard_map/ppermute | solution.py:220
  50.9 1.6 %collective-permute-start.7 = (bf16[64,2048]{1,0:T(8,128)(2,1)S(1)}, bf16[64,2048]{1,0:T(8,128)(2,1)}, u32[]{:S(2)}, u32[]{:S(2)}) collective-permute-start(bf16[64,2048]{1,0:T(8,128)(2,1)S(1)} %bitcast.27), channel_id=1, source_target_pairs={{0,8},{2,10},{4,12},{6,14},{8,0},{10,2},{12,4},{14,6},{16,24},{18,... | collective-permute-start | bytes 786440 | tf_op jit(solution)/shard_map/ppermute | solution.py:220
  52.7 2.4 %collective-permute-start.6 = (bf16[64,2048]{1,0:T(8,128)(2,1)S(1)}, bf16[64,2048]{1,0:T(8,128)(2,1)S(1)}, u32[]{:S(2)}, u32[]{:S(2)}) collective-permute-start(bf16[64,2048]{1,0:T(8,128)(2,1)S(1)} %bitcast.28), channel_id=1, source_target_pairs={{0,16},{2,18},{4,20},{6,22},{8,24},{10,26},{12,28},{14,30},{16,0},... | collective-permute-start | bytes 786440 | tf_op jit(solution)/shard_map/ppermute | solution.py:220
  55.1 6.9 %backward.3 = (bf16[640,4096]{1,0:T(8,128)(2,1)S(1)}, f32[576,256]{1,0:T(8,128)S(1)}, bf16[576,256]{1,0:T(8,128)(2,1)}, bf16[576,128]{1,0:T(8,128)(2,1)}) custom-call(bf16[640,640]{1,0:T(8,128)(2,1)S(1)} %get-tuple-element.44.rest_1_.c_ref, bf16[4096,640]{1,0:T(8,128)(2,1)S(1)} %bitcast.18, ...), custom_call_target="tpu_custom_call", output_to_operand_aliasing={{0}: (4, {})} | custom-call | flops 1090519040 | bytes 1000000 | tf_op jit(solution)/shard_map/backward/pallas_call | solution.py:450
  61.9 2.3 %copy-done = bf16[640,4096]{1,0:T(8,128)(2,1)} copy-done((bf16[640,4096]{1,0:T(8,128)(2,1)}, bf16[640,4096]{1,0:T(8,128)(2,1)S(1)}, u32[]{:S(2)}) %copy-start) | copy-done | bytes 5242904
  64.3 1.3 %collective-permute-start.8 = (bf16[576,256]{1,0:T(8,128)(2,1)}, bf16[576,256]{1,0:T(8,128)(2,1)S(1)}, u32[]{:S(2)}, u32[]{:S(2)}) collective-permute-start(bf16[576,256]{1,0:T(8,128)(2,1)} %get-tuple-element.67), channel_id=1, source_target_pairs={{2,0},{4,2},{6,4},{8,6},{10,8},{12,10},{14,12},{16,14},{18,16},{20... | collective-permute-start | bytes 884744 | tf_op jit(solution)/shard_map/ppermute | solution.py:215
  65.5 1.3 %collective-permute-start.9 = (bf16[576,128]{1,0:T(8,128)(2,1)}, bf16[576,128]{1,0:T(8,128)(2,1)}, u32[]{:S(2)}, u32[]{:S(2)}) collective-permute-start(bf16[576,128]{1,0:T(8,128)(2,1)} %get-tuple-element.68), channel_id=1, source_target_pairs={{4,0},{6,2},{8,4},{10,6},{12,8},{14,10},{16,12},{18,14},{20,16},{2... | collective-permute-start | bytes 442376 | tf_op jit(solution)/shard_map/ppermute | solution.py:215
  66.9 1.0 %halving.11 = (bf16[32,2048]{1,0:T(8,128)(2,1)S(1)}, f32[32,2048]{1,0:T(8,128)S(1)}) custom-call(s32[1]{0:T(128)} %bitcast.place_ref, f32[2,32,2048]{2,1,0:T(8,128)S(1)} %get-tuple-element.63.hold_ref, bf16[2,32,2048]{2,1,0:T(8,128)(2,1)} %bitcast.14.got_ref), custom_call_target="tpu_custom_call" | custom-call | flops 125000 | bytes 2000000 | tf_op jit(solution)/shard_map/halving/pallas_call | solution.py:273
  67.9 4.4 %collective-permute-start.11 = (bf16[32,2048]{1,0:T(8,128)(2,1)S(1)}, bf16[32,2048]{1,0:T(8,128)(2,1)S(1)}, u32[]{:S(2)}, u32[]{:S(2)}) collective-permute-start(bf16[32,2048]{1,0:T(8,128)(2,1)S(1)} %get-tuple-element.64.rest_1_), channel_id=1, source_target_pairs={{0,16},{2,18},{4,20},{6,22},{8,24},{10,26},{12,28},{14,30},{16,0},... | collective-permute-start | bytes 393224 | tf_op jit(solution)/shard_map/ppermute | solution.py:220
  72.3 0.8 collective-permute-start.10
  73.1 2.5 %copy-done.1 = bf16[640,4096]{1,0:T(8,128)(2,1)S(1)} copy-done((bf16[640,4096]{1,0:T(8,128)(2,1)S(1)}, bf16[640,4096]{1,0:T(8,128)(2,1)}, u32[]{:S(2)}) %copy-start.1) | copy-done | bytes 5242904
  75.6 3.6 %query_gradient.2 = (bf16[128,18432]{1,0:T(8,128)(2,1)}, f32[8,128]{1,0:T(8,128)S(1)}) custom-call(bf16[576,640]{1,0:T(8,128)(2,1)S(1)} %get-tuple-element.43.rest_0_.ct_ref, bf16[640,4096]{1,0:T(8,128)(2,1)S(1)} %copy-done.1, bf16[32,2048]{1,0:T(8,128)(2,1)S(1)} %get-tuple-element.62.rest_0_, bf16[32,2048]{1,0:T(8,128)(2,1)S(1)} %get-tuple-element.64.rest_1_), custom_call_target="tpu_custom_call" | custom-call | flops 629145600 | bytes 1000000 | tf_op jit(solution)/shard_map/query_gradient/pallas_call | solution.py:475
  79.2 1.0 %latent.1 = (bf16[576,128]{1,0:T(8,128)(2,1)S(1)}, f32[576,128]{1,0:T(8,128)S(1)}) custom-call(s32[1]{0:T(128)} %bitcast.15.side_ref, f32[576,256]{1,0:T(8,128)S(1)} %get-tuple-element.66.near_ref, bf16[576,256]{1,0:T(8,128)(2,1)S(1)} %collective-permute-done.8.got1_ref, bf16[576,128]{1,0:T(8,128)(2,1)} %collective-permute-done.9.got2_ref, ...), custom_call_target="tpu_custom_call" | custom-call | flops 125000 | bytes 2000000 | tf_op jit(solution)/shard_map/latent/pallas_call | solution.py:497
  80.2 1.6 %collective-permute-start.12 = (bf16[576,128]{1,0:T(8,128)(2,1)S(1)}, bf16[576,128]{1,0:T(8,128)(2,1)S(1)}, u32[]{:S(2)}, u32[]{:S(2)}) collective-permute-start(bf16[576,128]{1,0:T(8,128)(2,1)S(1)} %get-tuple-element.70.rest_1_), channel_id=1, source_target_pairs={{0,1},{1,0},{2,3},{3,2},{4,5},{5,4},{6,7},{7,6},{8,9},{9,8},{10,11... | collective-permute-start | bytes 442376 | tf_op jit(solution)/shard_map/ppermute | solution.py:220
  81.8 3.6 %query_gradient.3 = (bf16[128,18432]{1,0:T(8,128)(2,1)}, f32[8,128]{1,0:T(8,128)}) custom-call(bf16[576,640]{1,0:T(8,128)(2,1)S(1)} %get-tuple-element.43.rest_0_.ct_ref, bf16[640,4096]{1,0:T(8,128)(2,1)S(1)} %copy-done.1, bf16[128,18432]{1,0:T(8,128)(2,1)} %get-tuple-element.65.rest_0_, ...), custom_call_target="tpu_custom_call", output_to_operand_aliasing={{0}: (2, {})} | custom-call | flops 629145600 | bytes 1000000 | tf_op jit(solution)/shard_map/query_gradient/pallas_call | solution.py:475
  85.4 1.0 %final.1 = (f32[32,4096]{1,0:T(8,128)}, f32[576,128]{1,0:T(8,128)}) custom-call(f32[576,128]{1,0:T(8,128)S(1)} %get-tuple-element.72.hold_ref, bf16[576,128]{1,0:T(8,128)(2,1)S(1)} %collective-permute-done.12.got_ref, f32[32,2048]{1,0:T(8,128)S(1)} %get-tuple-element.73.refs_0_, bf16[32,2048]{1,0:T(8,128)(2,1)S(1)} %collective-permute-done.10.rest_2_.refs_1_, ...), custom_call_target="tpu_custom_call" | custom-call | flops 125000 | bytes 2000000 | tf_op jit(solution)/shard_map/final/pallas_call | solution.py:524
  (31 shorter events, 0.4 us)
Async XLA Ops:
  0.6 16.7 %collective-permute-start = (bf16[576,256]{1,0:T(8,128)(2,1)}, bf16[576,256]{1,0:T(8,128)(2,1)S(1)}, u32[]{:S(2)}, u32[]{:S(2)}) collective-permute-start(bf16[576,256]{1,0:T(8,128)(2,1)} %bitcast.30), channel_id=1, source_target_pairs={{0,2},{2,4},{4,6},{6,8},{8,10},{10,12},{12,14},{14,16},{16,18},{18... | collective-permute-start | bytes 884744 | tf_op jit(solution)/shard_map/ppermute | solution.py:215
  3.9 13.4 %collective-permute-start.1 = (bf16[576,128]{1,0:T(8,128)(2,1)S(1)}, bf16[576,128]{1,0:T(8,128)(2,1)S(1)}, u32[]{:S(2)}, u32[]{:S(2)}) collective-permute-start(bf16[576,128]{1,0:T(8,128)(2,1)S(1)} %slice.4), channel_id=1, source_target_pairs={{0,4},{2,6},{4,8},{6,10},{8,12},{10,14},{12,16},{14,18},{16,20},{1... | collective-permute-start | bytes 442376 | tf_op jit(solution)/shard_map/ppermute | solution.py:215
  8.4 9.0 %copy-start.4 = (bf16[128,4096]{1,0:T(8,128)(2,1)S(1)}, bf16[128,4096]{1,0:T(8,128)(2,1)}, u32[]{:S(2)}) copy-start(bf16[128,4096]{1,0:T(8,128)(2,1)} %rest_3_.1) | copy-start | bytes 3145732
  17.4 2.5 %copy-start.2 = (bf16[4096,640]{1,0:T(8,128)(2,1)S(1)}, bf16[4096,640]{1,0:T(8,128)(2,1)}, u32[]{:S(2)}) copy-start(bf16[4096,640]{1,0:T(8,128)(2,1)} %get-tuple-element.41.rest_3_.rest_2_.qs_ref) | copy-start | bytes 15728644
  19.9 1.0 %copy-start.5 = (f32[704,128]{1,0:T(8,128)S(1)}, f32[704,128]{1,0:T(8,128)}, u32[]{:S(2)}) copy-start(f32[704,128]{1,0:T(8,128)} %get-tuple-element.42.rest_5_.rest_4_.table_ref) | copy-start | bytes 1081348
  20.8 1.0 %copy-start.7 = (bf16[576,256]{1,0:T(8,128)(2,1)S(1)}, bf16[576,256]{1,0:T(8,128)(2,1)}, u32[]{:S(2)}) copy-start(bf16[576,256]{1,0:T(8,128)(2,1)} %get-tuple-element.40.rest_0_) | copy-start | bytes 884740
  27.3 12.7 %slice-start = ((s8[5242880]{0:T(1024)(128)(4,1)}), s8[4194304]{0:T(1024)(128)(4,1)S(1)}, s32[]{:S(2)}) async-start(s8[5242880]{0:T(1024)(128)(4,1)} %bitcast.17), calls=%async_computation | async-start | bytes 8388608
  27.3 12.7 %slice-start.1 = ((s8[5242880]{0:T(1024)(128)(4,1)}), s8[1048576]{0:T(1024)(128)(4,1)S(1)}, s32[]{:S(2)}) async-start(s8[5242880]{0:T(1024)(128)(4,1)} %bitcast.17), calls=%async_computation.1 | async-start | bytes 2097152
  27.3 12.7 %copy-start.6 = (f32[704,128]{1,0:T(8,128)S(1)}, f32[704,128]{1,0:T(8,128)}, u32[]{:S(2)}) copy-start(f32[704,128]{1,0:T(8,128)} %get-tuple-element.42.rest_5_.rest_4_.table_ref) | copy-start | bytes 1081348
  32.6 7.4 %copy-start.3 = (bf16[4096,512]{1,0:T(8,128)(2,1)S(1)}, bf16[4096,512]{1,0:T(8,128)(2,1)}, u32[]{:S(2)}) copy-start(bf16[4096,512]{1,0:T(8,128)(2,1)} %get-tuple-element.45.glat_ref) | copy-start | bytes 12582916
  32.6 3.7 %collective-permute-start.3 = (bf16[256,2048]{1,0:T(8,128)(2,1)S(1)}, bf16[256,2048]{1,0:T(8,128)(2,1)S(1)}, u32[]{:S(2)}, u32[]{:S(2)}) collective-permute-start(bf16[256,2048]{1,0:T(8,128)(2,1)S(1)} %get-tuple-element.52), channel_id=1, source_target_pairs={{0,2},{2,0},{4,6},{6,4},{8,10},{10,8},{12,14},{14,12},{16,18},{18,... | collective-permute-start | bytes 3145736 | tf_op jit(solution)/shard_map/ppermute | solution.py:220
  34.1 4.1 %collective-permute-start.2 = (bf16[256,2048]{1,0:T(8,128)(2,1)S(1)}, bf16[256,2048]{1,0:T(8,128)(2,1)S(1)}, u32[]{:S(2)}, u32[]{:S(2)}) collective-permute-start(bf16[256,2048]{1,0:T(8,128)(2,1)S(1)} %get-tuple-element.49), channel_id=1, source_target_pairs={{0,2},{2,0},{4,6},{6,4},{8,10},{10,8},{12,14},{14,12},{16,18},{18,... | collective-permute-start | bytes 3145736 | tf_op jit(solution)/shard_map/ppermute | solution.py:220
  36.6 14.3 %collective-permute-start.5 = (bf16[128,2048]{1,0:T(8,128)(2,1)S(1)}, bf16[128,2048]{1,0:T(8,128)(2,1)S(1)}, u32[]{:S(2)}, u32[]{:S(2)}) collective-permute-start(bf16[128,2048]{1,0:T(8,128)(2,1)S(1)} %bitcast.23), channel_id=1, source_target_pairs={{0,4},{2,6},{4,0},{6,2},{8,12},{10,14},{12,8},{14,10},{16,20},{18,... | collective-permute-start | bytes 1572872 | tf_op jit(solution)/shard_map/ppermute | solution.py:220
  38.4 14.2 %collective-permute-start.4 = (bf16[128,2048]{1,0:T(8,128)(2,1)S(1)}, bf16[128,2048]{1,0:T(8,128)(2,1)S(1)}, u32[]{:S(2)}, u32[]{:S(2)}) collective-permute-start(bf16[128,2048]{1,0:T(8,128)(2,1)S(1)} %bitcast.24), channel_id=1, source_target_pairs={{0,8},{2,10},{4,12},{6,14},{8,0},{10,2},{12,4},{14,6},{16,24},{18,... | collective-permute-start | bytes 1572872 | tf_op jit(solution)/shard_map/ppermute | solution.py:220
  50.9 15.9 %collective-permute-start.7 = (bf16[64,2048]{1,0:T(8,128)(2,1)S(1)}, bf16[64,2048]{1,0:T(8,128)(2,1)}, u32[]{:S(2)}, u32[]{:S(2)}) collective-permute-start(bf16[64,2048]{1,0:T(8,128)(2,1)S(1)} %bitcast.27), channel_id=1, source_target_pairs={{0,8},{2,10},{4,12},{6,14},{8,0},{10,2},{12,4},{14,6},{16,24},{18,... | collective-permute-start | bytes 786440 | tf_op jit(solution)/shard_map/ppermute | solution.py:220
  52.7 19.6 %collective-permute-start.6 = (bf16[64,2048]{1,0:T(8,128)(2,1)S(1)}, bf16[64,2048]{1,0:T(8,128)(2,1)S(1)}, u32[]{:S(2)}, u32[]{:S(2)}) collective-permute-start(bf16[64,2048]{1,0:T(8,128)(2,1)S(1)} %bitcast.28), channel_id=1, source_target_pairs={{0,16},{2,18},{4,20},{6,22},{8,24},{10,26},{12,28},{14,30},{16,0},... | collective-permute-start | bytes 786440 | tf_op jit(solution)/shard_map/ppermute | solution.py:220
  61.9 2.3 %copy-start = (bf16[640,4096]{1,0:T(8,128)(2,1)}, bf16[640,4096]{1,0:T(8,128)(2,1)S(1)}, u32[]{:S(2)}) copy-start(bf16[640,4096]{1,0:T(8,128)(2,1)S(1)} %get-tuple-element.60.ds_ref) | copy-start | bytes 15728644
  64.3 14.9 %collective-permute-start.8 = (bf16[576,256]{1,0:T(8,128)(2,1)}, bf16[576,256]{1,0:T(8,128)(2,1)S(1)}, u32[]{:S(2)}, u32[]{:S(2)}) collective-permute-start(bf16[576,256]{1,0:T(8,128)(2,1)} %get-tuple-element.67), channel_id=1, source_target_pairs={{2,0},{4,2},{6,4},{8,6},{10,8},{12,10},{14,12},{16,14},{18,16},{20... | collective-permute-start | bytes 884744 | tf_op jit(solution)/shard_map/ppermute | solution.py:215
  65.5 13.6 %collective-permute-start.9 = (bf16[576,128]{1,0:T(8,128)(2,1)}, bf16[576,128]{1,0:T(8,128)(2,1)}, u32[]{:S(2)}, u32[]{:S(2)}) collective-permute-start(bf16[576,128]{1,0:T(8,128)(2,1)} %get-tuple-element.68), channel_id=1, source_target_pairs={{4,0},{6,2},{8,4},{10,6},{12,8},{14,10},{16,12},{18,14},{20,16},{2... | collective-permute-start | bytes 442376 | tf_op jit(solution)/shard_map/ppermute | solution.py:215
  67.9 13.9 %collective-permute-start.11 = (bf16[32,2048]{1,0:T(8,128)(2,1)S(1)}, bf16[32,2048]{1,0:T(8,128)(2,1)S(1)}, u32[]{:S(2)}, u32[]{:S(2)}) collective-permute-start(bf16[32,2048]{1,0:T(8,128)(2,1)S(1)} %get-tuple-element.64.rest_1_), channel_id=1, source_target_pairs={{0,16},{2,18},{4,20},{6,22},{8,24},{10,26},{12,28},{14,30},{16,0},... | collective-permute-start | bytes 393224 | tf_op jit(solution)/shard_map/ppermute | solution.py:220
  72.3 9.5 %collective-permute-start.10 = (bf16[32,2048]{1,0:T(8,128)(2,1)S(1)}, bf16[32,2048]{1,0:T(8,128)(2,1)S(1)}, u32[]{:S(2)}, u32[]{:S(2)}) collective-permute-start(bf16[32,2048]{1,0:T(8,128)(2,1)S(1)} %get-tuple-element.62.rest_0_), channel_id=1, source_target_pairs={{0,4},{2,6},{4,0},{6,2},{8,12},{10,14},{12,8},{14,10},{16,20},{18,... | collective-permute-start | bytes 393224 | tf_op jit(solution)/shard_map/ppermute | solution.py:220
  73.1 2.5 %copy-start.1 = (bf16[640,4096]{1,0:T(8,128)(2,1)S(1)}, bf16[640,4096]{1,0:T(8,128)(2,1)}, u32[]{:S(2)}) copy-start(bf16[640,4096]{1,0:T(8,128)(2,1)} %copy-done) | copy-start | bytes 15728644
  80.2 5.2 %collective-permute-start.12 = (bf16[576,128]{1,0:T(8,128)(2,1)S(1)}, bf16[576,128]{1,0:T(8,128)(2,1)S(1)}, u32[]{:S(2)}, u32[]{:S(2)}) collective-permute-start(bf16[576,128]{1,0:T(8,128)(2,1)S(1)} %get-tuple-element.70.rest_1_), channel_id=1, source_target_pairs={{0,1},{1,0},{2,3},{3,2},{4,5},{5,4},{6,7},{7,6},{8,9},{9,8},{10,11... | collective-permute-start | bytes 442376 | tf_op jit(solution)/shard_map/ppermute | solution.py:220
where the time goes:
time: 86.8 us; the launch traced here: 86.3 us
  Pallas kernels  43.2 us (50%)
  starting transfers between devices  24.9 us (29%)
  local copies, waits for them, and re-layouts  10.2 us (12%)
  waiting for transfers between devices  7.22 us (8%)
    ppermute x9, starting transfers between devices, swapped(): lax.ppermute(value, axis, [(source, source ^ bit) for source in range(cou...  15.5 us
    pallas_call x2, Pallas kernels, on_device(): pl.pallas_call(functools.partial(backward_kernel, units=units, per_unit=u...  12.7 us
    pallas_call x2, Pallas kernels, on_device(): pl.pallas_call(functools.partial(forward_kernel, units=units, per_unit=un...  10.7 us
    ppermute x4, starting transfers between devices, passed_along(): lax.ppermute(value, axis, [(source, source + steps) for source in range(f...  9.35 us
    unnamed x20, local copies, waits for them, and re-layouts  9.26 us
    pallas_call x1, Pallas kernels, on_device(): pl.pallas_call(functools.partial(prepare_kernel, units=units, per_unit=un...  8.99 us
    ppermute x9, waiting for transfers between devices, swapped(): lax.ppermute(value, axis, [(source, source ^ bit) for source in range(cou...  7.21 us
    pallas_call x2, Pallas kernels, query_gradient(): pl.pallas_call(functools.partial(query_kernel, pairs=group // 2, rows=row...  7.14 us
  transfers between devices with their start and end apart: 13, of which 2 were waited for; matrix products, arithmetic and copies ran while one was open for 1% of the time, Pallas kernels for 37%

commit v1 on v0

--- a/solution.py
+++ b/solution.py
@@ -57,12 +57,11 @@
 
 
 def prepare_kernel(
-    place_ref, docs_ref, lat_ref, lse_ref, q_ref, g_ref, o_ref, w_ref,
-    own_ref, table_ref, qs_ref, glat_ref, *, units, per_unit, rows, feat, vdim, key_rows,
+    place_ref, docs_ref, lat_ref, lse_ref, g_ref, o_ref, w_ref, own_ref, table_ref, glat_ref,
+    *, units, per_unit, rows, vdim, key_rows,
 ):
     heads = lse_ref.shape[0]
     window = table_ref.shape[0] - 2 * heads
-    width = qs_ref.shape[1]
     span = per_unit * rows
 
     @pl.when(pl.program_id(0) == 0)
@@ -82,7 +81,6 @@
     deltas = []
     for unit in range(units):
         pairs = pairs_of(unit, per_unit)
-        qs_ref[unit * span : (unit + 1) * span, :] = wide_rows(q_ref, sum(pairs, []), feat, width)
         for i, pair in enumerate(pairs):
             row = unit * span + 2 * i * rows
             glat_ref[row : row + 2 * rows, :] = nt_dot(
@@ -101,9 +99,9 @@
     place_ref, *rest, units, per_unit, rows, feat, lat, vdim, base, own_rows, first, key_rows,
 ):
     if first:
-        (lat0_ref, lat1_ref, lat2_ref, qs_ref, g_ref, table_ref, p_ref, keep_ref, send_ref, ct_ref, c_ref) = rest
+        (lat0_ref, lat1_ref, lat2_ref, q_ref, g_ref, table_ref, p_ref, keep_ref, send_ref, ct_ref, c_ref) = rest
     else:
-        (ct_ref, c_ref, qs_ref, g_ref, table_ref, _, p_ref, keep_ref, send_ref) = rest
+        (ct_ref, c_ref, q_ref, g_ref, table_ref, _, p_ref, keep_ref, send_ref) = rest
     window, width = c_ref.shape
     far = window - key_rows
     core = place_ref[0] % 2
@@ -120,7 +118,9 @@
 
     bias = table_ref[:window, :]
     span = per_unit * rows
-    scores = [nt_dot(c_ref[...], qs_ref[unit * span : (unit + 1) * span, :]) for unit in range(units)]
+    scores = [
+        nt_dot(c_ref[...], wide_rows(q_ref, sum(pairs_of(unit, per_unit), []), feat, width)) for unit in range(units)
+    ]
     for unit in range(units):
         for k in range(per_unit):
             index = ((pl.program_id(0) + base) * units + unit) * per_unit + k
@@ -149,19 +149,27 @@
             )
 
 
+def store_turned(gq_ref, turned, first_head, count, rows, feat):
+    for k in range(0, count, 2):
+        both = jnp.concatenate(
+            [turned[:, (k + j) * rows : (k + j + 1) * rows] for j in range(2)], axis=0
+        )
+        gq_ref[:, (first_head + k) * feat : (first_head + k + 2) * feat] = both.T
+
+
 def backward_kernel(
-    c_ref, qs_ref, glat_ref, table_ref, p_ref, *rest,
+    ct_ref, c_ref, q_ref, glat_ref, table_ref, p_ref, *rest,
     units, per_unit, rows, feat, lat, steps, base, first, last, ties, key_rows,
 ):
     rest = list(rest)
     acc_in = None if first else rest.pop(0)
     rest = rest[ties:]
-    ds_ref = rest.pop(0)
     if last:
-        near_ref, far1_ref, far2_ref, acc = rest
+        ds_ref, near_ref, far1_ref, far2_ref, acc = rest
     else:
-        acc_out, acc = rest
+        gq_ref, acc_out, acc, ds_ref = rest
     span = per_unit * rows
+    width = c_ref.shape[1]
 
     @pl.when(pl.program_id(0) == 0)
     def _():
@@ -180,11 +188,16 @@
                 p_ref[:, own].astype(jnp.float32)
                 * ((gprobs[unit][:, k * rows : (k + 1) * rows] - delta) * softmax_scale)
             ).astype(jnp.bfloat16)
+    query = wide_rows(q_ref, list(range(units * per_unit)), feat, width)
     acc[:, :lat] += nn_dot(
         jnp.concatenate([ds_ref[...], p_ref[...]], axis=1),
-        jnp.concatenate([qs_ref[:, :lat], glat_ref[...]], axis=0),
+        jnp.concatenate([query[:, :lat], glat_ref[...]], axis=0),
     )
-    acc[:, lat:] += nn_dot(ds_ref[...], qs_ref[:, lat:])
+    acc[:, lat:] += nn_dot(ds_ref[...], query[:, lat:])
+    if not last:
+        for unit in range(units):
+            turned = nn_dot(ct_ref[...], ds_ref[:, unit * span : (unit + 1) * span]).astype(jnp.bfloat16)
+            store_turned(gq_ref, turned, unit * per_unit, per_unit, rows, feat)
 
     @pl.when(pl.program_id(0) == steps - 1)
     def _():
@@ -198,15 +211,10 @@
             acc_out[...] = acc[...]
 
 
-def query_kernel(ct_ref, ds_ref, *rest, pairs, rows, feat):
+def query_kernel(ct_ref, ds_ref, *rest, count, rows, feat):
     gq_ref, token_ref = rest[-2:]
     token_ref[...] = jnp.zeros_like(token_ref)
-    turned = nn_dot(ct_ref[...], ds_ref[...]).astype(jnp.bfloat16)
-    for i in range(pairs):
-        both = jnp.concatenate(
-            [turned[:, (2 * i + j) * rows : (2 * i + j + 1) * rows] for j in range(2)], axis=0
-        )
-        gq_ref[:, 2 * i * feat : 2 * (i + 1) * feat] = both.T
+    store_turned(gq_ref, nn_dot(ct_ref[...], ds_ref[...]).astype(jnp.bfloat16), 0, count, rows, feat)
 
 
 def passed_along(value, axis, steps):
@@ -225,7 +233,7 @@
 
 
 def cost(flops, moved):
-    return pl.CostEstimate(flops=int(flops / 8), bytes_accessed=int(moved), transcendentals=0)
+    return pl.CostEstimate(flops=int(flops), bytes_accessed=int(moved), transcendentals=0)
 
 
 def bit_of(place, bit):
@@ -314,9 +322,9 @@
     group = units * unit
     lanes = lambda i: (0, i)
     rowed = lambda i: (i, 0)
-    own, table, stacked, glat = pl.pallas_call(
+    own, table, glat = pl.pallas_call(
         functools.partial(
-            prepare_kernel, units=units, per_unit=unit, rows=rows, feat=feat, vdim=vdim, key_rows=key_rows
+            prepare_kernel, units=units, per_unit=unit, rows=rows, vdim=vdim, key_rows=key_rows
         ),
         grid=(heads // group,),
         in_specs=[
@@ -324,7 +332,6 @@
             smem,
             whole(feat, key_rows),
             whole(heads, rows),
-            pl.BlockSpec((rows, group * feat), lanes),
             pl.BlockSpec((rows, group * vdim), lanes),
             pl.BlockSpec((rows, group * vdim), lanes),
             pl.BlockSpec((lat, group * vdim), lanes),
@@ -332,19 +339,17 @@
         out_specs=[
             whole(feat, key_rows),
             whole(window + 2 * heads, rows),
-            pl.BlockSpec((group * rows, width), rowed),
             pl.BlockSpec((group * rows, lat), rowed),
         ],
         out_shape=[
             jax.ShapeDtypeStruct((feat, key_rows), jnp.bfloat16),
             jax.ShapeDtypeStruct((window + 2 * heads, rows), jnp.float32),
-            jax.ShapeDtypeStruct((heads * rows, width), jnp.bfloat16),
             jax.ShapeDtypeStruct((heads * rows, lat), jnp.bfloat16),
         ],
         compiler_params=params(prepare_bytes),
         cost_estimate=cost(heads * rows * 4 * lat * vdim, 20e6),
         name="prepare",
-    )(scalar, doc_starts, turned, sums_turned, queries, grad_out, out_saved, up_value)
+    )(scalar, doc_starts, turned, sums_turned, grad_out, out_saved, up_value)
 
     probs = None
     partials = []
@@ -365,11 +370,11 @@
             in_specs += [whole(feat, window), whole(window, width)]
             operands += [keys_turned, keys]
         in_specs += [
-            pl.BlockSpec((group * rows, width), rowed),
+            pl.BlockSpec((rows, group * feat), lanes),
             pl.BlockSpec((rows, group * vdim), lanes),
             whole(window + 2 * heads, rows),
         ]
-        operands += [stacked, grad_out, table]
+        operands += [queries, grad_out, table]
         halves = [pl.BlockSpec((lat // 2, group * vdim), lambda i: (0, i))] * 2
         out_specs = [pl.BlockSpec((window, group * rows), lanes)] + halves
         out_shape = [jax.ShapeDtypeStruct((window, heads * rows), jnp.bfloat16)]
@@ -423,21 +428,23 @@
         lanes = lambda i, base=base: (0, i + base)
         rowed = lambda i, base=base: (i + base, 0)
         in_specs = [
+            whole(feat, window),
             whole(window, width),
-            pl.BlockSpec((group * rows, width), rowed),
+            pl.BlockSpec((rows, group * feat), lanes),
             pl.BlockSpec((group * rows, lat), rowed),
             whole(window + 2 * heads, rows),
             pl.BlockSpec((window, group * rows), lanes),
         ]
-        operands = [keys, stacked, glat, table, probs]
+        operands = [keys_turned, keys, queries, glat, table, probs]
         if not first:
             in_specs.append(whole(window, width))
             operands.append(acc)
         in_specs += [untouched] * len(ties)
         operands += ties
-        out_specs = [pl.BlockSpec((window, group * rows), lanes)]
-        out_shape = [jax.ShapeDtypeStruct((window, heads * rows), jnp.bfloat16)]
+        scratch = [pltpu.VMEM((window, width), jnp.float32)]
         if last:
+            out_specs = [pl.BlockSpec((window, group * rows), lambda i: (0, i))]
+            out_shape = [jax.ShapeDtypeStruct((window, piece_heads * rows), jnp.bfloat16)]
             out_specs += [whole(feat, key_rows), whole(feat, key_rows), whole(feat, far - key_rows)]
             out_shape += [
                 jax.ShapeDtypeStruct((feat, key_rows), jnp.float32),
@@ -445,9 +452,13 @@
                 jax.ShapeDtypeStruct((feat, far - key_rows), jnp.bfloat16),
             ]
         else:
-            out_specs.append(whole(window, width))
-            out_shape.append(jax.ShapeDtypeStruct((window, width), jnp.float32))
-        probs, *rest = pl.pallas_call(
+            out_specs = [pl.BlockSpec((rows, group * feat), lanes), whole(window, width)]
+            out_shape = [
+                jax.ShapeDtypeStruct(queries.shape, jnp.bfloat16),
+                jax.ShapeDtypeStruct((window, width), jnp.float32),
+            ]
+            scratch.append(pltpu.VMEM((window, group * rows), jnp.bfloat16))
+        out = pl.pallas_call(
             functools.partial(
                 backward_kernel, units=units, per_unit=unit, rows=rows, feat=feat, lat=lat, base=base,
                 steps=steps, first=first, last=last, ties=len(ties), key_rows=key_rows,
@@ -456,41 +467,48 @@
             in_specs=in_specs,
             out_specs=out_specs,
             out_shape=out_shape,
-            scratch_shapes=[pltpu.VMEM((window, width), jnp.float32)],
-            input_output_aliases={4: 0},
+            scratch_shapes=scratch,
             compiler_params=params(),
             cost_estimate=cost(piece_heads * rows * 2 * window * (width + 2 * lat) * 2, 1e6),
             name="backward",
         )(*operands)
         if last:
-            near, far1, far2 = rest
+            dscores, near, far1, far2 = out
         else:
-            (acc,) = rest
-    dscores = probs
-
-    def query_gradient(piece, so_far, ties):
-        base = piece * steps
-        lanes = lambda i: (0, i + base)
-        extra = ([] if so_far is None else [so_far]) + ties
+            grad_queries, acc = out
+
+    late_heads = piece_heads // 2
+    late_group = min(4, late_heads)
+    late_steps = late_heads // late_group
+
+    def query_gradient(call, so_far, ties):
+        out_base = (heads - piece_heads + call * late_heads) // late_group
         return pl.pallas_call(
-            functools.partial(query_kernel, pairs=group // 2, rows=rows, feat=feat),
-            grid=(steps,),
-            in_specs=[whole(feat, window), pl.BlockSpec((window, group * rows), lanes)] + [untouched] * len(extra),
-            out_specs=[pl.BlockSpec((rows, group * feat), lanes), whole(8, 128)],
+            functools.partial(query_kernel, count=late_group, rows=rows, feat=feat),
+            grid=(late_steps,),
+            in_specs=[
+                whole(feat, window),
+                pl.BlockSpec((window, late_group * rows), lambda i: (0, call * late_steps + i)),
+            ]
+            + [untouched] * (1 + len(ties)),
+            out_specs=[
+                pl.BlockSpec((rows, late_group * feat), lambda i: (0, out_base + i)),
+                whole(8, 128),
+            ],
             out_shape=[
                 jax.ShapeDtypeStruct(queries.shape, jnp.bfloat16),
                 jax.ShapeDtypeStruct((8, 128), jnp.float32),
             ],
-            input_output_aliases={} if so_far is None else {2: 0},
+            input_output_aliases={2: 0},
             compiler_params=params(),
-            cost_estimate=cost(piece_heads * rows * 2 * window * width * 3, 1e6),
+            cost_estimate=cost(late_heads * rows * 2 * window * width * 3, 1e6),
             name="query_gradient",
-        )(keys_turned, dscores, *extra)
+        )(keys_turned, dscores, so_far, *ties)
 
     got1 = passed_along(far1, "ctx", -1)
     got2 = passed_along(far2, "ctx", -2)
     ties = [halving.step() for halving in halvings if halving.order]
-    grad_queries, token = query_gradient(0, None, ties)
+    grad_queries, token = query_gradient(0, grad_queries, ties)
     position = lax.axis_index("head").astype(jnp.int32)
     bit = lax.axis_size("head") // 2
     part = key_rows // 2

time: 86.8 us -> 82.2 us (0.947)
  Pallas kernels: 43.2 us -> 39.6 us
    pallas_call x2, Pallas kernels: 12.7 us -> 15.2 us  [on_device(): pl.pallas_call(functools.partial(backward_kernel, units=units, per_unit=u...]
    pallas_call x2, Pallas kernels: 7.14 us -> 4.76 us  [query_gradient(): pl.pallas_call(functools.partial(query_kernel, count=late_group, rows=row...]
    pallas_call x1, Pallas kernels: 8.99 us -> 6.63 us  [on_device(): pl.pallas_call(functools.partial(prepare_kernel, units=units, per_unit=un...]
    pallas_call x6, Pallas kernels: 1.67 us -> 0.7 us  [step(): pl.pallas_call(functools.partial(halving_kernel, dim=self.opened.index(bi...]
    pallas_call x1, Pallas kernels: 1.01 us -> 0.1 us  [on_device(): pl.pallas_call(latent_kernel, in_specs=[smem] + [pl.BlockSpec(memory_spac...]
    unnamed x20 -> x24, local copies, waits for them, and re-layouts: 9.26 us -> 8.79 us
  transfers between devices with their start and end apart: 13 -> 13, of which waited for: 2 -> 3; matrix products, arithmetic and copies ran while one was open for 1% -> 1% of each run, Pallas kernels for 37% -> 33%
where the time goes in v1:
time: 82.2 us; the launch traced here: 81.8 us
  Pallas kernels  39.6 us (48%)
  starting transfers between devices  25.1 us (31%)
  local copies, waits for them, and re-layouts  9.72 us (12%)
  waiting for transfers between devices  6.55 us (8%)
  between operations  0.85 us (1%)
    ppermute x9, starting transfers between devices, swapped(): lax.ppermute(value, axis, [(source, source ^ bit) for source in range(cou...  15.6 us
    pallas_call x2, Pallas kernels, on_device(): pl.pallas_call(functools.partial(backward_kernel, units=units, per_unit=u...  15.2 us
    pallas_call x2, Pallas kernels, on_device(): pl.pallas_call(functools.partial(forward_kernel, units=units, per_unit=un...  11.3 us
    ppermute x4, starting transfers between devices, passed_along(): lax.ppermute(value, axis, [(source, source + steps) for source in range(f...  9.48 us
    unnamed x24, local copies, waits for them, and re-layouts  8.79 us
    pallas_call x1, Pallas kernels, on_device(): pl.pallas_call(functools.partial(prepare_kernel, units=units, per_unit=un...  6.63 us
    ppermute x9, waiting for transfers between devices, swapped(): lax.ppermute(value, axis, [(source, source ^ bit) for source in range(cou...  6.54 us
    pallas_call x2, Pallas kernels, query_gradient(): pl.pallas_call(functools.partial(query_kernel, count=late_group, rows=row...  4.76 us
  transfers between devices with their start and end apart: 13, of which 3 were waited for; matrix products, arithmetic and copies ran while one was open for 1% of the time, Pallas kernels for 33%

profile of v1, /device:TPU:0, one launch (start us, length us, event | category | flops | bytes accessed | tf_op | source)
XLA Modules:
  0.0 81.8 jit_solution(5746998656415475148)
XLA Ops:
  0.6 2.5 %collective-permute-start = (bf16[576,256]{1,0:T(8,128)(2,1)}, bf16[576,256]{1,0:T(8,128)(2,1)S(1)}, u32[]{:S(2)}, u32[]{:S(2)}) collective-permute-start(bf16[576,256]{1,0:T(8,128)(2,1)} %bitcast.29), channel_id=1, source_target_pairs={{0,2},{2,4},{4,6},{6,8},{8,10},{10,12},{12,14},{14,16},{16,18},{18... | collective-permute-start | bytes 884744 | tf_op jit(solution)/shard_map/ppermute | solution.py:223
  3.2 0.9 %slice.4 = bf16[576,128]{1,0:T(8,128)(2,1)S(1)} slice(bf16[576,256]{1,0:T(8,128)(2,1)} %bitcast.30), slice={[0:576], [128:256]} | slice | bytes 294912 | tf_op jit(solution)/shard_map/slice | solution.py:310
  4.1 4.4 %collective-permute-start.1 = (bf16[576,128]{1,0:T(8,128)(2,1)S(1)}, bf16[576,128]{1,0:T(8,128)(2,1)S(1)}, u32[]{:S(2)}, u32[]{:S(2)}) collective-permute-start(bf16[576,128]{1,0:T(8,128)(2,1)S(1)} %slice.4), channel_id=1, source_target_pairs={{0,4},{2,6},{4,8},{6,10},{8,12},{10,14},{12,16},{14,18},{16,20},{1... | collective-permute-start | bytes 442376 | tf_op jit(solution)/shard_map/ppermute | solution.py:223
  8.5 6.6 %prepare.1 = (bf16[576,256]{1,0:T(8,128)(2,1)}, f32[704,128]{1,0:T(8,128)}, bf16[4096,512]{1,0:T(8,128)(2,1)}) custom-call(s32[1]{0:T(128)} %bitcast.place_ref, s32[65]{0:T(128)} %docs_ref.1, bf16[576,256]{1,0:T(8,128)(2,1)} %bitcast.31, f32[32,128]{1,0:T(8,128)} %bitcast.32, bf16[128,4096]{1,0:T(8,128)(2,1)} %rest_3_.3, bf16[128,4096]{1,0:T(8,128)(2,1)} %o_ref.1, ...), custom_call_target="tpu_custom_call" | custom-call | flops 1073741824 | bytes 20000000 | tf_op jit(solution)/shard_map/prepare/pallas_call | solution.py:325
  15.2 1.0 %copy-done.3 = f32[704,128]{1,0:T(8,128)S(1)} copy-done((f32[704,128]{1,0:T(8,128)S(1)}, f32[704,128]{1,0:T(8,128)}, u32[]{:S(2)}) %copy-start.3) | copy-done | bytes 360472
  16.2 1.0 %copy-done.5 = bf16[576,256]{1,0:T(8,128)(2,1)S(1)} copy-done((bf16[576,256]{1,0:T(8,128)(2,1)S(1)}, bf16[576,256]{1,0:T(8,128)(2,1)}, u32[]{:S(2)}) %copy-start.5) | copy-done | bytes 294936
  17.1 5.8 %forward.2 = (bf16[640,4096]{1,0:T(8,128)(2,1)S(1)}, bf16[256,2048]{1,0:T(8,128)(2,1)S(1)}, bf16[256,2048]{1,0:T(8,128)(2,1)S(1)}, bf16[576,640]{1,0:T(8,128)(2,1)S(1)}, bf16[640,640]{1,0:T(8,128)(2,1)S(1)}) custom-call(s32[1]{0:T(128)} %bitcast.place_ref, bf16[576,256]{1,0:T(8,128)(2,1)S(1)} %copy-done.5, ...), custom_call_target="tpu_custom_call" | custom-call | flops 6039797760 | bytes 1000000 | tf_op jit(solution)/shard_map/forward/pallas_call | solution.py:393
  23.0 5.5 %forward.3 = (bf16[640,4096]{1,0:T(8,128)(2,1)S(1)}, bf16[256,2048]{1,0:T(8,128)(2,1)S(1)}, bf16[256,2048]{1,0:T(8,128)(2,1)S(1)}) custom-call(s32[1]{0:T(128)} %bitcast.place_ref, bf16[576,640]{1,0:T(8,128)(2,1)S(1)} %get-tuple-element.41.rest_0_.ct_ref, bf16[640,640]{1,0:T(8,128)(2,1)S(1)} %get-tuple-element.42.rest_1_.c_ref, ...), custom_call_target="tpu_custom_call", output_to_operand_aliasing={{0}: (6, {})} | custom-call | flops 6039797760 | bytes 1000000 | tf_op jit(solution)/shard_map/forward/pallas_call | solution.py:393
  28.4 1.4 %collective-permute-start.3 = (bf16[256,2048]{1,0:T(8,128)(2,1)S(1)}, bf16[256,2048]{1,0:T(8,128)(2,1)S(1)}, u32[]{:S(2)}, u32[]{:S(2)}) collective-permute-start(bf16[256,2048]{1,0:T(8,128)(2,1)S(1)} %get-tuple-element.50), channel_id=1, source_target_pairs={{0,2},{2,0},{4,6},{6,4},{8,10},{10,8},{12,14},{14,12},{16,18},{18,... | collective-permute-start | bytes 3145736 | tf_op jit(solution)/shard_map/ppermute | solution.py:228
  30.0 2.2 %collective-permute-done.3 = bf16[256,2048]{1,0:T(8,128)(2,1)S(1)} collective-permute-done((bf16[256,2048]{1,0:T(8,128)(2,1)S(1)}, bf16[256,2048]{1,0:T(8,128)(2,1)S(1)}, u32[]{:S(2)}, u32[]{:S(2)}) %collective-permute-start.3) | collective-permute-done | bytes 1048608 | tf_op jit(solution)/shard_map/ppermute | solution.py:228
  32.2 0.2 halving.7
  32.4 1.6 %collective-permute-start.5 = (bf16[128,2048]{1,0:T(8,128)(2,1)S(1)}, bf16[128,2048]{1,0:T(8,128)(2,1)S(1)}, u32[]{:S(2)}, u32[]{:S(2)}) collective-permute-start(bf16[128,2048]{1,0:T(8,128)(2,1)S(1)} %bitcast.25), channel_id=1, source_target_pairs={{0,4},{2,6},{4,0},{6,2},{8,12},{10,14},{12,8},{14,10},{16,20},{18,... | collective-permute-start | bytes 1572872 | tf_op jit(solution)/shard_map/ppermute | solution.py:228
  34.0 0.2 halving.6
  34.2 1.7 %collective-permute-start.4 = (bf16[128,2048]{1,0:T(8,128)(2,1)S(1)}, bf16[128,2048]{1,0:T(8,128)(2,1)S(1)}, u32[]{:S(2)}, u32[]{:S(2)}) collective-permute-start(bf16[128,2048]{1,0:T(8,128)(2,1)S(1)} %bitcast.26), channel_id=1, source_target_pairs={{0,8},{2,10},{4,12},{6,14},{8,0},{10,2},{12,4},{14,6},{16,24},{18,... | collective-permute-start | bytes 1572872 | tf_op jit(solution)/shard_map/ppermute | solution.py:228
  35.9 8.9 %backward.2 = (bf16[128,18432]{1,0:T(8,128)(2,1)}, f32[640,640]{1,0:T(8,128)S(1)}) custom-call(bf16[576,640]{1,0:T(8,128)(2,1)S(1)} %get-tuple-element.41.rest_0_.ct_ref, bf16[640,640]{1,0:T(8,128)(2,1)S(1)} %get-tuple-element.42.rest_1_.c_ref, bf16[128,18432]{1,0:T(8,128)(2,1)S(1)} %copy-done.1, bf16[4096,512]{1,0:T(8,128)(2,1)S(1)} %copy-done.2, ...), custom_call_target="tpu_custom_call" | custom-call | flops 8724152320 | bytes 1000000 | tf_op jit(solution)/shard_map/backward/pallas_call | solution.py:461
  44.7 2.0 %collective-permute-done.5 = bf16[128,2048]{1,0:T(8,128)(2,1)S(1)} collective-permute-done((bf16[128,2048]{1,0:T(8,128)(2,1)S(1)}, bf16[128,2048]{1,0:T(8,128)(2,1)S(1)}, u32[]{:S(2)}, u32[]{:S(2)}) %collective-permute-start.5) | collective-permute-done | bytes 524320 | tf_op jit(solution)/shard_map/ppermute | solution.py:228
  46.8 1.6 %collective-permute-start.7 = (bf16[64,2048]{1,0:T(8,128)(2,1)S(1)}, bf16[64,2048]{1,0:T(8,128)(2,1)S(1)}, u32[]{:S(2)}, u32[]{:S(2)}) collective-permute-start(bf16[64,2048]{1,0:T(8,128)(2,1)S(1)} %bitcast.27), channel_id=1, source_target_pairs={{0,8},{2,10},{4,12},{6,14},{8,0},{10,2},{12,4},{14,6},{16,24},{18,... | collective-permute-start | bytes 786440 | tf_op jit(solution)/shard_map/ppermute | solution.py:228
  48.5 2.4 %collective-permute-start.6 = (bf16[64,2048]{1,0:T(8,128)(2,1)S(1)}, bf16[64,2048]{1,0:T(8,128)(2,1)S(1)}, u32[]{:S(2)}, u32[]{:S(2)}) collective-permute-start(bf16[64,2048]{1,0:T(8,128)(2,1)S(1)} %bitcast.28), channel_id=1, source_target_pairs={{0,16},{2,18},{4,20},{6,22},{8,24},{10,26},{12,28},{14,30},{16,0},... | collective-permute-start | bytes 786440 | tf_op jit(solution)/shard_map/ppermute | solution.py:228
  50.9 2.5 %copy-done.11 = bf16[640,4096]{1,0:T(8,128)(2,1)S(1)} copy-done((bf16[640,4096]{1,0:T(8,128)(2,1)S(1)}, bf16[640,4096]{1,0:T(8,128)(2,1)}, u32[]{:S(2)}) %copy-start.11) | copy-done | bytes 5242904
  53.4 6.3 %backward.3 = (bf16[640,2048]{1,0:T(8,128)(2,1)S(1)}, f32[576,256]{1,0:T(8,128)S(1)}, bf16[576,256]{1,0:T(8,128)(2,1)S(1)}, bf16[576,128]{1,0:T(8,128)(2,1)S(1)}) custom-call(bf16[576,640]{1,0:T(8,128)(2,1)S(1)} %get-tuple-element.41.rest_0_.ct_ref, bf16[640,640]{1,0:T(8,128)(2,1)S(1)} %get-tuple-element.42.rest_1_.c_ref, bf16[128,18432]{1,0:T(8,128)(2,1)S(1)} %copy-done.1, ...), custom_call_target="tpu_custom_call" | custom-call | flops 8724152320 | bytes 1000000 | tf_op jit(solution)/shard_map/backward/pallas_call | solution.py:461
  59.7 1.5 %copy-done.6 = bf16[640,2048]{1,0:T(8,128)(2,1)} copy-done((bf16[640,2048]{1,0:T(8,128)(2,1)}, bf16[640,2048]{1,0:T(8,128)(2,1)S(1)}, u32[]{:S(2)}) %copy-start.6) | copy-done | bytes 2621464
  61.2 1.3 %collective-permute-start.8 = (bf16[576,256]{1,0:T(8,128)(2,1)S(1)}, bf16[576,256]{1,0:T(8,128)(2,1)S(1)}, u32[]{:S(2)}, u32[]{:S(2)}) collective-permute-start(bf16[576,256]{1,0:T(8,128)(2,1)S(1)} %get-tuple-element.65), channel_id=1, source_target_pairs={{2,0},{4,2},{6,4},{8,6},{10,8},{12,10},{14,12},{16,14},{18,16},{20... | collective-permute-start | bytes 884744 | tf_op jit(solution)/shard_map/ppermute | solution.py:223
  62.5 1.3 %collective-permute-start.9 = (bf16[576,128]{1,0:T(8,128)(2,1)S(1)}, bf16[576,128]{1,0:T(8,128)(2,1)S(1)}, u32[]{:S(2)}, u32[]{:S(2)}) collective-permute-start(bf16[576,128]{1,0:T(8,128)(2,1)S(1)} %get-tuple-element.66), channel_id=1, source_target_pairs={{4,0},{6,2},{8,4},{10,6},{12,8},{14,10},{16,12},{18,14},{20,16},{2... | collective-permute-start | bytes 442376 | tf_op jit(solution)/shard_map/ppermute | solution.py:223
  63.9 4.4 %collective-permute-start.11 = (bf16[32,2048]{1,0:T(8,128)(2,1)S(1)}, bf16[32,2048]{1,0:T(8,128)(2,1)S(1)}, u32[]{:S(2)}, u32[]{:S(2)}) collective-permute-start(bf16[32,2048]{1,0:T(8,128)(2,1)S(1)} %get-tuple-element.62.rest_2_), channel_id=1, source_target_pairs={{0,16},{2,18},{4,20},{6,22},{8,24},{10,26},{12,28},{14,30},{16,0},... | collective-permute-start | bytes 393224 | tf_op jit(solution)/shard_map/ppermute | solution.py:228
  68.3 0.8 collective-permute-start.10
  69.1 1.7 %copy-done.7 = bf16[640,2048]{1,0:T(8,128)(2,1)S(1)} copy-done((bf16[640,2048]{1,0:T(8,128)(2,1)S(1)}, bf16[640,2048]{1,0:T(8,128)(2,1)}, u32[]{:S(2)}) %copy-start.7) | copy-done | bytes 2621464
  70.8 1.1 %copy-done.9 = bf16[576,640]{1,0:T(8,128)(2,1)S(1)} copy-done((bf16[576,640]{1,0:T(8,128)(2,1)S(1)}, bf16[576,640]{1,0:T(8,128)(2,1)}, u32[]{:S(2)}) %copy-start.9) | copy-done | bytes 737304
  72.0 2.4 %query_gradient.2 = (bf16[128,18432]{1,0:T(8,128)(2,1)}, f32[8,128]{1,0:T(8,128)S(1)}) custom-call(bf16[576,640]{1,0:T(8,128)(2,1)S(1)} %copy-done.9, bf16[640,2048]{1,0:T(8,128)(2,1)S(1)} %copy-done.7, bf16[128,18432]{1,0:T(8,128)(2,1)} %get-tuple-element.58.rest_0_, ...), custom_call_target="tpu_custom_call", output_to_operand_aliasing={{0}: (2, {})} | custom-call | flops 2516582400 | bytes 1000000 | tf_op jit(solution)/shard_map/query_gradient/pallas_call | solution.py:486
  74.5 1.6 %collective-permute-start.12 = (bf16[576,128]{1,0:T(8,128)(2,1)S(1)}, bf16[576,128]{1,0:T(8,128)(2,1)S(1)}, u32[]{:S(2)}, u32[]{:S(2)}) collective-permute-start(bf16[576,128]{1,0:T(8,128)(2,1)S(1)} %get-tuple-element.68.rest_1_), channel_id=1, source_target_pairs={{0,1},{1,0},{2,3},{3,2},{4,5},{5,4},{6,7},{7,6},{8,9},{9,8},{10,11... | collective-permute-start | bytes 442376 | tf_op jit(solution)/shard_map/ppermute | solution.py:228
  76.0 2.4 %collective-permute-done.11.rest_3_.refs_3_ = bf16[32,2048]{1,0:T(8,128)(2,1)S(1)} collective-permute-done((bf16[32,2048]{1,0:T(8,128)(2,1)S(1)}, bf16[32,2048]{1,0:T(8,128)(2,1)S(1)}, u32[]{:S(2)}, u32[]{:S(2)}) %collective-permute-start.11) | collective-permute-done | bytes 131104 | tf_op jit(solution)/shard_map/ppermute | solution.py:228
  78.4 2.4 %query_gradient.3 = (bf16[128,18432]{1,0:T(8,128)(2,1)}, f32[8,128]{1,0:T(8,128)}) custom-call(bf16[576,640]{1,0:T(8,128)(2,1)S(1)} %copy-done.9, bf16[640,2048]{1,0:T(8,128)(2,1)S(1)} %copy-done.7, bf16[128,18432]{1,0:T(8,128)(2,1)} %get-tuple-element.63.rest_0_, bf16[576,128]{1,0:T(8,128)(2,1)S(1)} %get-tuple-element.68.rest_1_, ...), custom_call_target="tpu_custom_call", output_to_operand_aliasing={{0}: (2, {})} | custom-call | flops 2516582400 | bytes 1000000 | tf_op jit(solution)/shard_map/query_gradient/pallas_call | solution.py:486
  80.8 1.0 %final.1 = (f32[32,4096]{1,0:T(8,128)}, f32[576,128]{1,0:T(8,128)}) custom-call(f32[576,128]{1,0:T(8,128)S(1)} %get-tuple-element.70.hold_ref, bf16[576,128]{1,0:T(8,128)(2,1)S(1)} %collective-permute-done.12.got_ref, f32[32,2048]{1,0:T(8,128)S(1)} %get-tuple-element.71.refs_0_, bf16[32,2048]{1,0:T(8,128)(2,1)S(1)} %collective-permute-done.10.rest_2_.refs_1_, ...), custom_call_target="tpu_custom_call" | custom-call | flops 1000000 | bytes 2000000 | tf_op jit(solution)/shard_map/final/pallas_call | solution.py:542
  (34 shorter events, 0.5 us)
Async XLA Ops:
  0.6 14.5 %copy-start = (bf16[128,4096]{1,0:T(8,128)(2,1)S(1)}, bf16[128,4096]{1,0:T(8,128)(2,1)}, u32[]{:S(2)}) copy-start(bf16[128,4096]{1,0:T(8,128)(2,1)} %rest_3_.3) | copy-start | bytes 3145732
  0.6 14.5 %collective-permute-start = (bf16[576,256]{1,0:T(8,128)(2,1)}, bf16[576,256]{1,0:T(8,128)(2,1)S(1)}, u32[]{:S(2)}, u32[]{:S(2)}) collective-permute-start(bf16[576,256]{1,0:T(8,128)(2,1)} %bitcast.29), channel_id=1, source_target_pairs={{0,2},{2,4},{4,6},{6,8},{8,10},{10,12},{12,14},{14,16},{16,18},{18... | collective-permute-start | bytes 884744 | tf_op jit(solution)/shard_map/ppermute | solution.py:223
  4.1 11.1 %collective-permute-start.1 = (bf16[576,128]{1,0:T(8,128)(2,1)S(1)}, bf16[576,128]{1,0:T(8,128)(2,1)S(1)}, u32[]{:S(2)}, u32[]{:S(2)}) collective-permute-start(bf16[576,128]{1,0:T(8,128)(2,1)S(1)} %slice.4), channel_id=1, source_target_pairs={{0,4},{2,6},{4,8},{6,10},{8,12},{10,14},{12,16},{14,18},{16,20},{1... | collective-permute-start | bytes 442376 | tf_op jit(solution)/shard_map/ppermute | solution.py:223
  8.5 6.7 %copy-start.1 = (bf16[128,18432]{1,0:T(8,128)(2,1)S(1)}, bf16[128,18432]{1,0:T(8,128)(2,1)}, u32[]{:S(2)}) copy-start(bf16[128,18432]{1,0:T(8,128)(2,1)} %q_ref.3) | copy-start | bytes 14155780
  15.2 1.0 %copy-start.3 = (f32[704,128]{1,0:T(8,128)S(1)}, f32[704,128]{1,0:T(8,128)}, u32[]{:S(2)}) copy-start(f32[704,128]{1,0:T(8,128)} %get-tuple-element.40.rest_5_.rest_4_.table_ref) | copy-start | bytes 1081348
  16.2 1.0 %copy-start.5 = (bf16[576,256]{1,0:T(8,128)(2,1)S(1)}, bf16[576,256]{1,0:T(8,128)(2,1)}, u32[]{:S(2)}) copy-start(bf16[576,256]{1,0:T(8,128)(2,1)} %get-tuple-element.39.rest_0_) | copy-start | bytes 884740
  17.1 5.8 %copy-start.4 = (f32[704,128]{1,0:T(8,128)S(1)}, f32[704,128]{1,0:T(8,128)}, u32[]{:S(2)}) copy-start(f32[704,128]{1,0:T(8,128)} %get-tuple-element.40.rest_5_.rest_4_.table_ref) | copy-start | bytes 1081348
  22.9 28.0 %copy-start.8 = (bf16[576,640]{1,0:T(8,128)(2,1)}, bf16[576,640]{1,0:T(8,128)(2,1)S(1)}, u32[]{:S(2)}) copy-start(bf16[576,640]{1,0:T(8,128)(2,1)S(1)} %get-tuple-element.41.rest_0_.ct_ref) | copy-start | bytes 2211844
  22.9 12.9 %copy-start.2 = (bf16[4096,512]{1,0:T(8,128)(2,1)S(1)}, bf16[4096,512]{1,0:T(8,128)(2,1)}, u32[]{:S(2)}) copy-start(bf16[4096,512]{1,0:T(8,128)(2,1)} %get-tuple-element.43.glat_ref) | copy-start | bytes 12582916
  28.4 16.3 %copy-start.10 = (bf16[640,4096]{1,0:T(8,128)(2,1)}, bf16[640,4096]{1,0:T(8,128)(2,1)S(1)}, u32[]{:S(2)}) copy-start(bf16[640,4096]{1,0:T(8,128)(2,1)S(1)} %get-tuple-element.45.p_ref) | copy-start | bytes 15728644
  28.4 3.7 %collective-permute-start.3 = (bf16[256,2048]{1,0:T(8,128)(2,1)S(1)}, bf16[256,2048]{1,0:T(8,128)(2,1)S(1)}, u32[]{:S(2)}, u32[]{:S(2)}) collective-permute-start(bf16[256,2048]{1,0:T(8,128)(2,1)S(1)} %get-tuple-element.50), channel_id=1, source_target_pairs={{0,2},{2,0},{4,6},{6,4},{8,10},{10,8},{12,14},{14,12},{16,18},{18,... | collective-permute-start | bytes 3145736 | tf_op jit(solution)/shard_map/ppermute | solution.py:228
  29.9 4.1 %collective-permute-start.2 = (bf16[256,2048]{1,0:T(8,128)(2,1)S(1)}, bf16[256,2048]{1,0:T(8,128)(2,1)S(1)}, u32[]{:S(2)}, u32[]{:S(2)}) collective-permute-start(bf16[256,2048]{1,0:T(8,128)(2,1)S(1)} %get-tuple-element.47), channel_id=1, source_target_pairs={{0,2},{2,0},{4,6},{6,4},{8,10},{10,8},{12,14},{14,12},{16,18},{18,... | collective-permute-start | bytes 3145736 | tf_op jit(solution)/shard_map/ppermute | solution.py:228
  32.4 14.3 %collective-permute-start.5 = (bf16[128,2048]{1,0:T(8,128)(2,1)S(1)}, bf16[128,2048]{1,0:T(8,128)(2,1)S(1)}, u32[]{:S(2)}, u32[]{:S(2)}) collective-permute-start(bf16[128,2048]{1,0:T(8,128)(2,1)S(1)} %bitcast.25), channel_id=1, source_target_pairs={{0,4},{2,6},{4,0},{6,2},{8,12},{10,14},{12,8},{14,10},{16,20},{18,... | collective-permute-start | bytes 1572872 | tf_op jit(solution)/shard_map/ppermute | solution.py:228
  34.2 14.2 %collective-permute-start.4 = (bf16[128,2048]{1,0:T(8,128)(2,1)S(1)}, bf16[128,2048]{1,0:T(8,128)(2,1)S(1)}, u32[]{:S(2)}, u32[]{:S(2)}) collective-permute-start(bf16[128,2048]{1,0:T(8,128)(2,1)S(1)} %bitcast.26), channel_id=1, source_target_pairs={{0,8},{2,10},{4,12},{6,14},{8,0},{10,2},{12,4},{14,6},{16,24},{18,... | collective-permute-start | bytes 1572872 | tf_op jit(solution)/shard_map/ppermute | solution.py:228
  46.8 17.1 %collective-permute-start.7 = (bf16[64,2048]{1,0:T(8,128)(2,1)S(1)}, bf16[64,2048]{1,0:T(8,128)(2,1)S(1)}, u32[]{:S(2)}, u32[]{:S(2)}) collective-permute-start(bf16[64,2048]{1,0:T(8,128)(2,1)S(1)} %bitcast.27), channel_id=1, source_target_pairs={{0,8},{2,10},{4,12},{6,14},{8,0},{10,2},{12,4},{14,6},{16,24},{18,... | collective-permute-start | bytes 786440 | tf_op jit(solution)/shard_map/ppermute | solution.py:228
  48.5 19.8 %collective-permute-start.6 = (bf16[64,2048]{1,0:T(8,128)(2,1)S(1)}, bf16[64,2048]{1,0:T(8,128)(2,1)S(1)}, u32[]{:S(2)}, u32[]{:S(2)}) collective-permute-start(bf16[64,2048]{1,0:T(8,128)(2,1)S(1)} %bitcast.28), channel_id=1, source_target_pairs={{0,16},{2,18},{4,20},{6,22},{8,24},{10,26},{12,28},{14,30},{16,0},... | collective-permute-start | bytes 786440 | tf_op jit(solution)/shard_map/ppermute | solution.py:228
  50.9 2.5 %copy-start.11 = (bf16[640,4096]{1,0:T(8,128)(2,1)S(1)}, bf16[640,4096]{1,0:T(8,128)(2,1)}, u32[]{:S(2)}) copy-start(bf16[640,4096]{1,0:T(8,128)(2,1)} %copy-done.10) | copy-start | bytes 15728644
  59.7 1.5 %copy-start.6 = (bf16[640,2048]{1,0:T(8,128)(2,1)}, bf16[640,2048]{1,0:T(8,128)(2,1)S(1)}, u32[]{:S(2)}) copy-start(bf16[640,2048]{1,0:T(8,128)(2,1)S(1)} %get-tuple-element.57.ds_ref) | copy-start | bytes 7864324
  61.2 13.1 %collective-permute-start.8 = (bf16[576,256]{1,0:T(8,128)(2,1)S(1)}, bf16[576,256]{1,0:T(8,128)(2,1)S(1)}, u32[]{:S(2)}, u32[]{:S(2)}) collective-permute-start(bf16[576,256]{1,0:T(8,128)(2,1)S(1)} %get-tuple-element.65), channel_id=1, source_target_pairs={{2,0},{4,2},{6,4},{8,6},{10,8},{12,10},{14,12},{16,14},{18,16},{20... | collective-permute-start | bytes 884744 | tf_op jit(solution)/shard_map/ppermute | solution.py:223
  62.5 11.8 %collective-permute-start.9 = (bf16[576,128]{1,0:T(8,128)(2,1)S(1)}, bf16[576,128]{1,0:T(8,128)(2,1)S(1)}, u32[]{:S(2)}, u32[]{:S(2)}) collective-permute-start(bf16[576,128]{1,0:T(8,128)(2,1)S(1)} %get-tuple-element.66), channel_id=1, source_target_pairs={{4,0},{6,2},{8,4},{10,6},{12,8},{14,10},{16,12},{18,14},{20,16},{2... | collective-permute-start | bytes 442376 | tf_op jit(solution)/shard_map/ppermute | solution.py:223
  63.9 14.5 %collective-permute-start.11 = (bf16[32,2048]{1,0:T(8,128)(2,1)S(1)}, bf16[32,2048]{1,0:T(8,128)(2,1)S(1)}, u32[]{:S(2)}, u32[]{:S(2)}) collective-permute-start(bf16[32,2048]{1,0:T(8,128)(2,1)S(1)} %get-tuple-element.62.rest_2_), channel_id=1, source_target_pairs={{0,16},{2,18},{4,20},{6,22},{8,24},{10,26},{12,28},{14,30},{16,0},... | collective-permute-start | bytes 393224 | tf_op jit(solution)/shard_map/ppermute | solution.py:228
  68.3 10.1 %collective-permute-start.10 = (bf16[32,2048]{1,0:T(8,128)(2,1)S(1)}, bf16[32,2048]{1,0:T(8,128)(2,1)S(1)}, u32[]{:S(2)}, u32[]{:S(2)}) collective-permute-start(bf16[32,2048]{1,0:T(8,128)(2,1)S(1)} %get-tuple-element.60.rest_1_), channel_id=1, source_target_pairs={{0,4},{2,6},{4,0},{6,2},{8,12},{10,14},{12,8},{14,10},{16,20},{18,... | collective-permute-start | bytes 393224 | tf_op jit(solution)/shard_map/ppermute | solution.py:228
  69.1 1.7 %copy-start.7 = (bf16[640,2048]{1,0:T(8,128)(2,1)S(1)}, bf16[640,2048]{1,0:T(8,128)(2,1)}, u32[]{:S(2)}) copy-start(bf16[640,2048]{1,0:T(8,128)(2,1)} %copy-done.6) | copy-start | bytes 7864324
  70.8 1.1 %copy-start.9 = (bf16[576,640]{1,0:T(8,128)(2,1)S(1)}, bf16[576,640]{1,0:T(8,128)(2,1)}, u32[]{:S(2)}) copy-start(bf16[576,640]{1,0:T(8,128)(2,1)} %copy-done.8) | copy-start | bytes 2211844
  74.5 6.3 %collective-permute-start.12 = (bf16[576,128]{1,0:T(8,128)(2,1)S(1)}, bf16[576,128]{1,0:T(8,128)(2,1)S(1)}, u32[]{:S(2)}, u32[]{:S(2)}) collective-permute-start(bf16[576,128]{1,0:T(8,128)(2,1)S(1)} %get-tuple-element.68.rest_1_), channel_id=1, source_target_pairs={{0,1},{1,0},{2,3},{3,2},{4,5},{5,4},{6,7},{7,6},{8,9},{9,8},{10,11... | collective-permute-start | bytes 442376 | tf_op jit(solution)/shard_map/ppermute | solution.py:228
